TPU v7x, 32 devices: a whole 2x2x4 slice. The times are simulated.
32 devices in a mesh: dp: 8 (over z, x), tensor: 4 (over y, core).
Axes of the slice: x: 2, y: 2, z: 4, core: 2. Of those that a mesh axis runs over, the one named last changes fastest.
Arguments:
- tokens: bfloat16 [16, 1024, 768], P('dp', 'tensor'), may hold values from -6 to 6
- w_qkv: bfloat16 [2, 768, 3, 768], P(None, 'dp', None, 'tensor'), may hold values from -0.21875 to 0.21875
- w_out: bfloat16 [2, 768, 768], P(None, 'tensor', 'dp'), may hold values from -0.875 to 0.875
- w_up: bfloat16 [2, 768, 3072], P(None, 'dp', 'tensor'), may hold values from -0.21875 to 0.21875
- w_down: bfloat16 [2, 3072, 768], P(None, 'tensor', 'dp'), may hold values from -0.109375 to 0.109375
- norm_gain: bfloat16 [2, 2, 768], P(None, None, 'dp'), may hold values from 0.5 to 1.5
- norm_bias: bfloat16 [2, 2, 768], P(None, None, 'dp'), may hold values from -1.5 to 1.5
- seg_table: bfloat16 [8, 768], P(None, 'dp'), may hold values from -4 to 4
- seg_ids: int32 [16, 8], P('dp', 'tensor'), may hold values from 0 to 7
- cotangent: bfloat16 [16, 1024, 768], P('dp', 'tensor'), may hold values from -6 to 6
Outputs:
- result: bfloat16 [16, 1024, 768], P('dp', 'tensor')
- grad_tokens: float32 [16, 1024, 768], P('dp', 'tensor')
- grad_qkv: float32 [2, 768, 3, 768], P(None, 'dp', None, 'tensor')
- grad_out: float32 [2, 768, 768], P(None, 'tensor', 'dp')
- grad_up: float32 [2, 768, 3072], P(None, 'dp', 'tensor')
- grad_down: float32 [2, 3072, 768], P(None, 'tensor', 'dp')
- grad_gain: float32 [2, 2, 768], P(None, None, 'dp')
- grad_bias: float32 [2, 2, 768], P(None, None, 'dp')
- grad_table: float32 [8, 768], P(None, 'dp')
Inputs may be any that keep to these rules, and one draw needn't show every extreme that they name: `seg_ids`: one table row for each segment.
All inputs are finite; a program needn't handle non-finite values.
Results may differ from a plain program's by a relative error of at most 0.025.
Values may be sent and summed in bfloat16 or wider, within the bound.
No kernel may reach another device: no remote copies, remote signals or barrier semaphores. Data moves between devices by JAX's collectives and lax.ppermute only.
A program may use at most 128 MiB of HBM per device.

v0:
```python
import jax
import jax.numpy as jnp
from jax import lax
from jax.sharding import PartitionSpec as P

HEAD_DIM = 64
SEG = 128
NSEG = 8


highest = lax.Precision.HIGHEST


def layer_norm(hidden, gain_row, offset):
    center = hidden - jnp.mean(hidden, axis=-1, keepdims=True)
    spread = jnp.mean(center * center, axis=-1, keepdims=True)
    return center * lax.rsqrt(spread + 1e-05) * gain_row + offset


def exact_gelu(upward):
    return jax.nn.gelu(upward, approximate=False)


def spread_rows(values):
    return lax.all_gather(values, "tensor", axis=0, tiled=True)


def collect_rows(partial_value):
    return lax.psum_scatter(partial_value, "tensor", scatter_dimension=0, tiled=True)


def spread_grads(values):
    return lax.all_gather(values, "tensor", axis=0, tiled=True)


def collect_grads(partial_value):
    return lax.psum_scatter(
        partial_value.astype(jnp.bfloat16), "tensor", scatter_dimension=0, tiled=True
    ).astype(jnp.float32)


def fetch_weights(shards):
    return (
        lax.all_gather(shards[0], "dp", axis=1, tiled=True),
        lax.all_gather(shards[1], "dp", axis=2, tiled=True),
        lax.all_gather(shards[2], "dp", axis=1, tiled=True),
        lax.all_gather(shards[3], "dp", axis=2, tiled=True),
        lax.all_gather(shards[4], "dp", axis=2, tiled=True),
        lax.all_gather(shards[5], "dp", axis=2, tiled=True),
        lax.all_gather(shards[6], "dp", axis=1, tiled=True),
    )


def reduce_grads(local_grads):
    return (
        lax.psum_scatter(local_grads[0], "dp", scatter_dimension=1, tiled=True),
        lax.psum_scatter(local_grads[1], "dp", scatter_dimension=2, tiled=True),
        lax.psum_scatter(local_grads[2], "dp", scatter_dimension=1, tiled=True),
        lax.psum_scatter(local_grads[3], "dp", scatter_dimension=2, tiled=True),
        lax.psum_scatter(local_grads[4], "dp", scatter_dimension=2, tiled=True),
        lax.psum_scatter(local_grads[5], "dp", scatter_dimension=2, tiled=True),
        lax.psum_scatter(local_grads[6], "dp", scatter_dimension=1, tiled=True),
    )


def split_heads(project, group_len):
    row_count = project.shape[0]
    head_count = project.shape[2] // HEAD_DIM
    shaped = project.reshape(row_count // group_len, group_len, 3, head_count, HEAD_DIM)
    return (shaped[:, :, 0], shaped[:, :, 1], shaped[:, :, 2])


def attention_scores(queries, key_rows):
    return jnp.einsum(
        "nqhe,nkhe->nhqk", queries, key_rows, preferred_element_type=jnp.float32
    ) * HEAD_DIM ** (-0.5)


def block_forward(hidden_in, weights, group_len):
    w_qkv, w_out, w_up, w_down, gains, offsets = weights
    sent = spread_rows(hidden_in.astype(jnp.bfloat16))
    row_count = sent.shape[0]
    project = jnp.einsum("rd,dch->rch", sent, w_qkv, preferred_element_type=jnp.float32).astype(
        jnp.bfloat16
    )
    queries, key_rows, values = split_heads(project, group_len)
    scores = attention_scores(queries, key_rows)
    top_score = jnp.max(scores, axis=-1, keepdims=True)
    log_total = top_score + jnp.log(jnp.sum(jnp.exp(scores - top_score), axis=-1, keepdims=True))
    probs = jnp.exp(scores - log_total)
    context = jnp.einsum(
        "nhqk,nkhe->nqhe", probs.astype(jnp.bfloat16), values, preferred_element_type=jnp.float32
    )
    context = context.reshape(row_count, project.shape[2]).astype(jnp.bfloat16)
    attended = collect_rows(jnp.dot(context, w_out, preferred_element_type=jnp.float32))
    normed, first_back = jax.vjp(layer_norm, hidden_in + attended, gains[0], offsets[0])
    normed_sent = spread_rows(normed.astype(jnp.bfloat16))
    upward = jnp.dot(normed_sent, w_up, preferred_element_type=jnp.float32)
    activated, gelu_back = jax.vjp(exact_gelu, upward)
    activated_low = activated.astype(jnp.bfloat16)
    mlp_out = collect_rows(jnp.dot(activated_low, w_down, preferred_element_type=jnp.float32))
    output, second_back = jax.vjp(layer_norm, normed + mlp_out, gains[1], offsets[1])
    kept = (
        sent,
        project,
        log_total,
        context,
        normed_sent,
        activated_low,
        first_back,
        gelu_back,
        second_back,
    )
    return (output, kept)


def block_backward(grad_output, weights, kept, group_len):
    w_qkv, w_out, w_up, w_down, gains, offsets = weights
    (
        sent,
        project,
        log_total,
        context,
        normed_sent,
        activated_low,
        first_back,
        gelu_back,
        second_back,
    ) = kept
    row_count = sent.shape[0]
    grad_second, gain_second, offset_second = second_back(grad_output)
    grad_mlp = spread_grads(grad_second.astype(jnp.bfloat16))
    grad_downw = jnp.einsum(
        "rf,rd->fd", activated_low, grad_mlp, preferred_element_type=jnp.float32
    )
    grad_active = jnp.einsum("rd,fd->rf", grad_mlp, w_down, preferred_element_type=jnp.float32)
    (grad_upward,) = gelu_back(grad_active)
    grad_up_low = grad_upward.astype(jnp.bfloat16)
    grad_upw = jnp.einsum("rd,rf->df", normed_sent, grad_up_low, preferred_element_type=jnp.float32)
    grad_normed = grad_second + collect_grads(
        jnp.einsum("rf,df->rd", grad_up_low, w_up, preferred_element_type=jnp.float32)
    )
    grad_first, gain_first, offset_first = first_back(grad_normed)
    grad_branch = spread_grads(grad_first.astype(jnp.bfloat16))
    grad_outw = jnp.einsum("rk,rd->kd", context, grad_branch, preferred_element_type=jnp.float32)
    grad_context = jnp.einsum(
        "rd,kd->rk", grad_branch, w_out, preferred_element_type=jnp.float32
    ).astype(jnp.bfloat16)
    queries, key_rows, values = split_heads(project, group_len)
    probs = jnp.exp(attention_scores(queries, key_rows) - log_total)
    grad_groups = grad_context.reshape(queries.shape)
    grad_values = jnp.einsum(
        "nhqk,nqhe->nkhe",
        probs.astype(jnp.bfloat16),
        grad_groups,
        preferred_element_type=jnp.float32,
    )
    grad_probs = jnp.einsum(
        "nqhe,nkhe->nhqk", grad_groups, values, preferred_element_type=jnp.float32
    )
    grad_scores = (
        probs * (grad_probs - jnp.sum(probs * grad_probs, axis=-1, keepdims=True))
    ).astype(jnp.bfloat16)
    grad_queries = jnp.einsum(
        "nhqk,nkhe->nqhe", grad_scores, key_rows, preferred_element_type=jnp.float32
    ) * HEAD_DIM ** (-0.5)
    grad_keys = jnp.einsum(
        "nhqk,nqhe->nkhe", grad_scores, queries, preferred_element_type=jnp.float32
    ) * HEAD_DIM ** (-0.5)
    local_width = project.shape[2]
    grad_project = jnp.stack(
        [
            grad_queries.reshape(row_count, local_width),
            grad_keys.reshape(row_count, local_width),
            grad_values.reshape(row_count, local_width),
        ],
        axis=1,
    ).astype(jnp.bfloat16)
    grad_qkvw = jnp.einsum("rd,rch->dch", sent, grad_project, preferred_element_type=jnp.float32)
    grad_input = grad_first + collect_grads(
        jnp.einsum("rch,dch->rd", grad_project, w_qkv, preferred_element_type=jnp.float32)
    )
    grads = (
        grad_qkvw,
        grad_outw,
        grad_upw,
        grad_downw,
        jnp.stack([gain_first, gain_second]),
        jnp.stack([offset_first, offset_second]),
    )
    return (grad_input, grads)


def micro_step(weights_all, token_rows, grad_rows, segment_ids):
    w_qkv, w_out, w_up, w_down, gains, offsets, table = weights_all
    first_qkv, first_out, first_up, first_down = (w_qkv[0], w_out[0], w_up[0], w_down[0])
    segment_weights = (
        first_qkv,
        first_out,
        first_up,
        first_down,
        gains[0].astype(jnp.float32),
        offsets[0].astype(jnp.float32),
    )
    cross_weights = (
        w_qkv[1],
        w_out[1],
        w_up[1],
        w_down[1],
        gains[1].astype(jnp.float32),
        offsets[1].astype(jnp.float32),
    )
    segment_out, segment_kept = block_forward(token_rows.astype(jnp.float32), segment_weights, SEG)
    onehot = (segment_ids[:, None] == jnp.arange(table.shape[0], dtype=jnp.int32)[None, :]).astype(
        jnp.float32
    )
    placed = segment_out[::SEG] + jnp.dot(onehot, table.astype(jnp.float32), precision=highest)
    cross_out, cross_kept = block_forward(placed, cross_weights, NSEG)
    layer_out = segment_out.at[::SEG].set(cross_out).astype(jnp.bfloat16)
    grad_whole = grad_rows.astype(jnp.float32)
    grad_placed, cross_grads = block_backward(grad_whole[::SEG], cross_weights, cross_kept, NSEG)
    grad_table = jnp.dot(onehot.T, grad_placed, precision=highest)
    grad_segment = grad_whole.at[::SEG].set(grad_placed)
    grad_input, segment_grads = block_backward(grad_segment, segment_weights, segment_kept, SEG)
    local_grads = tuple(
        (
            jnp.stack([first_part, second_part])
            for first_part, second_part in zip(segment_grads, cross_grads)
        )
    ) + (grad_table,)
    return (layer_out, grad_input, local_grads)


def body(tokens, w_qkv, w_out, w_up, w_down, norm_gain, norm_bias, seg_table, seg_ids, cotangent):
    shards = (w_qkv, w_out, w_up, w_down, norm_gain, norm_bias, seg_table)
    dp_count = lax.axis_size("dp")
    shapes = [
        (2, w_qkv.shape[1] * dp_count, 3, w_qkv.shape[3]),
        (2, w_out.shape[1], w_out.shape[2] * dp_count),
        (2, w_up.shape[1] * dp_count, w_up.shape[2]),
        (2, w_down.shape[1], w_down.shape[2] * dp_count),
        (2, 2, norm_gain.shape[2] * dp_count),
        (2, 2, norm_bias.shape[2] * dp_count),
        (seg_table.shape[0], seg_table.shape[1] * dp_count),
    ]
    zeros = tuple((jnp.zeros(shape_item, jnp.float32) for shape_item in shapes))

    def step(totals, items):
        token_rows, grad_rows, segment_ids = items
        weights_now = fetch_weights(shards)
        layer_out, grad_input, local_grads = micro_step(
            weights_now, token_rows, grad_rows, segment_ids
        )
        totals = tuple((total + part for total, part in zip(totals, local_grads)))
        return (totals, (layer_out, grad_input))

    totals, (results, grad_tokens) = lax.scan(step, zeros, (tokens, cotangent, seg_ids))
    totals = reduce_grads(totals)
    grad_gain, grad_bias, grad_table = lax.psum((totals[4], totals[5], totals[6]), "tensor")
    return (
        results,
        grad_tokens,
        totals[0],
        totals[1],
        totals[2],
        totals[3],
        grad_gain,
        grad_bias,
        grad_table,
    )


def solution(mesh):
    return jax.shard_map(
        body,
        mesh=mesh,
        in_specs=(
            P("dp", "tensor", None),
            P(None, "dp", None, "tensor"),
            P(None, "tensor", "dp"),
            P(None, "dp", "tensor"),
            P(None, "tensor", "dp"),
            P(None, None, "dp"),
            P(None, None, "dp"),
            P(None, "dp"),
            P("dp", "tensor"),
            P("dp", "tensor", None),
        ),
        out_specs=(
            P("dp", "tensor", None),
            P("dp", "tensor", None),
            P(None, "dp", None, "tensor"),
            P(None, "tensor", "dp"),
            P(None, "dp", "tensor"),
            P(None, "tensor", "dp"),
            P(None, None, "dp"),
            P(None, None, "dp"),
            P(None, "dp"),
        ),
        check_vma=False,
    )
```

profile of v0, /device:TPU:0, one launch (start us, length us, event | category | flops | bytes accessed | tf_op | source)
XLA Modules:
  0.0 1673.1 jit_solution(16861145227729946429)
XLA Ops:
  13.9 1095.7 %while.27 = (s32[]{:T(128)}, f32[2,768,3,192]{1,3,2,0:T(8,128)}, f32[2,192,768]{2,1,0:T(8,128)}, f32[2,768,768]{2,1,0:T(8,128)}, f32[2,768,768]{2,1,0:T(8,128)},...) while((s32[]{:T(128)}, f32[2,768,3,192]{1,3,2,0:T(8,128)}, ...), condition=%wide.region_41.42_spmd.clone, body=%wide.region_0.41_spmd.clone.sunk | while | flops 11356053504 | bytes 400070720 | solution.py:257
  16.6 34.7 %all_gather.64 = bf16[2,192,768]{1,0,2:T(2,128)(2,1)S(1)} all-gather(bf16[2,192,96]{1,0,2:T(2,128)(2,1)S(1)} %get-tuple-element.703), channel_id=1, replica_groups=mesh['dp'=8,'tensor'=4] {'dp'}, dimensions={2}, use_global_device_ids=true | all-gather | bytes 663552 | tf_op jit(solution)/shard_map/while/body/eval_jaxpr/all_gather | solution.py:45
  53.7 21.2 %all-gather.32.cloned.1.call-done = bf16[2,768,3,192]{3,0,2,1:T(2,128)(2,1)} async-done(((bf16[2,96,3,192]{3,0,2,1:T(2,128)(2,1)}), bf16[2,768,3,192]{3,0,2,1:T(2,128)(2,1)}) %all-gather.32.cloned.1.call-update) | async-done | bytes 1769488 | tf_op jit(solution)/shard_map/while/body/eval_jaxpr/all_gather | solution.py:44
  74.9 8.7 fusion.268
  83.6 5.4 copy.262
  89.0 6.3 all-gather.34.cloned.1.call-done
  103.6 31.4 %all_gather.65 = bf16[2,2,768]{1,0,2:T(2,128)(2,1)S(1)} all-gather(bf16[2,2,96]{1,0,2:T(2,128)(2,1)} %get-tuple-element.704), channel_id=1, replica_groups=mesh['dp'=8,'tensor'=4] {'dp'}, dimensions={2}, use_global_device_ids=true | all-gather | bytes 6912 | tf_op jit(solution)/shard_map/while/body/eval_jaxpr/all_gather | solution.py:49
  135.0 31.7 %all_gather.66 = bf16[2,2,768]{1,0,2:T(2,128)(2,1)S(1)} all-gather(bf16[2,2,96]{1,0,2:T(2,128)(2,1)} %get-tuple-element.702), channel_id=1, replica_groups=mesh['dp'=8,'tensor'=4] {'dp'}, dimensions={2}, use_global_device_ids=true | all-gather | bytes 6912 | tf_op jit(solution)/shard_map/while/body/eval_jaxpr/all_gather | solution.py:48
  182.0 13.8 all-gather.38.cloned.1.call-done
  195.8 20.3 %all-gather.36.cloned.1.call-done = bf16[1024,768]{1,0:T(8,128)(2,1)} async-done(((bf16[256,768]{1,0:T(8,128)(2,1)}), bf16[1024,768]{1,0:T(8,128)(2,1)}) %all-gather.36.cloned.1.call-update) | async-done | bytes 1572880 | tf_op jit(solution)/shard_map/while/body/eval_jaxpr/all_gather | solution.py:25
  216.1 11.6 multiply_convert_fusion.13
  227.7 42.8 %all-gather.40.cloned.1.call-done = bf16[2,768,768]{1,2,0:T(8,128)(2,1)} async-done(((bf16[2,768,96]{1,2,0:T(8,128)(2,1)}), bf16[2,768,768]{1,2,0:T(8,128)(2,1)}) %all-gather.40.cloned.1.call-update) | async-done | bytes 2359312 | tf_op jit(solution)/shard_map/while/body/eval_jaxpr/all_gather | solution.py:47
  275.9 26.4 %all-gather.19 = bf16[8,96,8]{1,2,0:T(8,128)(2,1)S(1)} all-gather(bf16[1,96,8]{1,2,0:T(8,128)(2,1)S(1)} %bitcast.471), channel_id=1, replica_groups=mesh['dp'=8,'tensor'=4] {'dp'}, dimensions={0}, use_global_device_ids=true | all-gather | bytes 13824 | tf_op jit(solution)/shard_map/while/body/eval_jaxpr/all_gather | solution.py:50
  316.4 6.3 slice_reduce_fusion.15
  322.7 6.4 copy.267
  341.2 11.5 all-reduce.9
  354.4 5.2 all-gather.21
  363.5 11.8 all-reduce.10
  380.0 5.6 all-gather.22
  391.4 12.6 all-reduce.11
  407.5 5.3 all-gather.23
  418.9 10.4 all-reduce.12
  437.6 17.0 %all-gather.42.cloned.1.call-done = bf16[1024,768]{1,0:T(8,128)(2,1)} async-done(((bf16[256,768]{1,0:T(8,128)(2,1)}), bf16[1024,768]{1,0:T(8,128)(2,1)}) %all-gather.42.cloned.1.call-update) | async-done | bytes 1572880 | tf_op jit(solution)/shard_map/while/body/eval_jaxpr/all_gather | solution.py:33
  454.6 5.8 add_convert_fusion.12
  464.3 28.3 %reduce-scatter.38.cloned.1.call-done = bf16[256,768]{1,0:T(8,128)(2,1)} async-done(((bf16[1024,768]{1,0:T(8,128)(2,1)}), bf16[256,768]{1,0:T(8,128)(2,1)}) %reduce-scatter.38.cloned.1.call-update) | async-done | bytes 393232 | tf_op jit(solution)/shard_map/while/body/eval_jaxpr/reduce_scatter | solution.py:37
  507.0 10.2 all-gather.44.cloned.1.call-done
  547.4 11.5 reduce-scatter.40.cloned.1.call-done
  563.8 32.9 %all_gather.64 = bf16[2,192,768]{1,0,2:T(2,128)(2,1)S(1)} all-gather(bf16[2,192,96]{1,0,2:T(2,128)(2,1)S(1)} %get-tuple-element.703), channel_id=1, replica_groups=mesh['dp'=8,'tensor'=4] {'dp'}, dimensions={2}, use_global_device_ids=true | all-gather | bytes 663552 | tf_op jit(solution)/shard_map/while/body/eval_jaxpr/all_gather | solution.py:45
  599.2 20.4 %all-gather.32.cloned.1.call-done = bf16[2,768,3,192]{3,0,2,1:T(2,128)(2,1)} async-done(((bf16[2,96,3,192]{3,0,2,1:T(2,128)(2,1)}), bf16[2,768,3,192]{3,0,2,1:T(2,128)(2,1)}) %all-gather.32.cloned.1.call-update) | async-done | bytes 1769488 | tf_op jit(solution)/shard_map/while/body/eval_jaxpr/all_gather | solution.py:44
  619.6 8.7 fusion.268
  628.2 5.4 copy.262
  633.7 6.3 all-gather.34.cloned.1.call-done
  648.2 31.4 %all_gather.65 = bf16[2,2,768]{1,0,2:T(2,128)(2,1)S(1)} all-gather(bf16[2,2,96]{1,0,2:T(2,128)(2,1)} %get-tuple-element.704), channel_id=1, replica_groups=mesh['dp'=8,'tensor'=4] {'dp'}, dimensions={2}, use_global_device_ids=true | all-gather | bytes 6912 | tf_op jit(solution)/shard_map/while/body/eval_jaxpr/all_gather | solution.py:49
  679.6 31.7 %all_gather.66 = bf16[2,2,768]{1,0,2:T(2,128)(2,1)S(1)} all-gather(bf16[2,2,96]{1,0,2:T(2,128)(2,1)} %get-tuple-element.702), channel_id=1, replica_groups=mesh['dp'=8,'tensor'=4] {'dp'}, dimensions={2}, use_global_device_ids=true | all-gather | bytes 6912 | tf_op jit(solution)/shard_map/while/body/eval_jaxpr/all_gather | solution.py:48
  726.6 13.8 all-gather.38.cloned.1.call-done
  740.4 20.3 %all-gather.36.cloned.1.call-done = bf16[1024,768]{1,0:T(8,128)(2,1)} async-done(((bf16[256,768]{1,0:T(8,128)(2,1)}), bf16[1024,768]{1,0:T(8,128)(2,1)}) %all-gather.36.cloned.1.call-update) | async-done | bytes 1572880 | tf_op jit(solution)/shard_map/while/body/eval_jaxpr/all_gather | solution.py:25
  760.7 11.6 multiply_convert_fusion.13
  772.3 42.8 %all-gather.40.cloned.1.call-done = bf16[2,768,768]{1,2,0:T(8,128)(2,1)} async-done(((bf16[2,768,96]{1,2,0:T(8,128)(2,1)}), bf16[2,768,768]{1,2,0:T(8,128)(2,1)}) %all-gather.40.cloned.1.call-update) | async-done | bytes 2359312 | tf_op jit(solution)/shard_map/while/body/eval_jaxpr/all_gather | solution.py:47
  820.6 26.4 %all-gather.19 = bf16[8,96,8]{1,2,0:T(8,128)(2,1)S(1)} all-gather(bf16[1,96,8]{1,2,0:T(8,128)(2,1)S(1)} %bitcast.471), channel_id=1, replica_groups=mesh['dp'=8,'tensor'=4] {'dp'}, dimensions={0}, use_global_device_ids=true | all-gather | bytes 13824 | tf_op jit(solution)/shard_map/while/body/eval_jaxpr/all_gather | solution.py:50
  861.1 6.3 slice_reduce_fusion.15
  867.3 6.4 copy.267
  885.9 11.5 all-reduce.9
  899.0 5.2 all-gather.21
  908.1 11.8 all-reduce.10
  924.7 5.6 all-gather.22
  936.1 12.6 all-reduce.11
  952.2 5.3 all-gather.23
  963.6 10.4 all-reduce.12
  982.2 17.0 %all-gather.42.cloned.1.call-done = bf16[1024,768]{1,0:T(8,128)(2,1)} async-done(((bf16[256,768]{1,0:T(8,128)(2,1)}), bf16[1024,768]{1,0:T(8,128)(2,1)}) %all-gather.42.cloned.1.call-update) | async-done | bytes 1572880 | tf_op jit(solution)/shard_map/while/body/eval_jaxpr/all_gather | solution.py:33
  999.2 5.8 add_convert_fusion.12
  1009.0 28.3 %reduce-scatter.38.cloned.1.call-done = bf16[256,768]{1,0:T(8,128)(2,1)} async-done(((bf16[1024,768]{1,0:T(8,128)(2,1)}), bf16[256,768]{1,0:T(8,128)(2,1)}) %reduce-scatter.38.cloned.1.call-update) | async-done | bytes 393232 | tf_op jit(solution)/shard_map/while/body/eval_jaxpr/reduce_scatter | solution.py:37
  1051.6 10.2 all-gather.44.cloned.1.call-done
  1081.4 7.6 maximum_add_fusion.12
  1097.0 6.6 reduce-scatter.40.cloned.1.call-done
  1118.1 5.6 copy.132
  1124.5 6.1 copy.133
  1130.6 44.3 %reduce-scatter.28.cloned.1.call-done = f32[96,4]{1,0:T(8,128)} async-done(((f32[768,4]{1,0:T(8,128)}), f32[96,4]{1,0:T(8,128)}) %reduce-scatter.28.cloned.1.call-update) | async-done | bytes 1552
  1175.9 62.7 %reduce-scatter.30.cloned.1.call-done = f32[96,4]{1,0:T(8,128)} async-done(((f32[768,4]{1,0:T(8,128)}), f32[96,4]{1,0:T(8,128)}) %reduce-scatter.30.cloned.1.call-update) | async-done | bytes 1552
  1239.6 62.7 %reduce-scatter.32.cloned.1.call-done = f32[96,8]{1,0:T(8,128)} async-done(((f32[768,8]{1,0:T(8,128)}), f32[96,8]{1,0:T(8,128)}) %reduce-scatter.32.cloned.1.call-update) | async-done | bytes 3088
  1303.2 6.3 all-reduce.4
  1309.5 59.4 %reduce-scatter.26.cloned.1.call-done = f32[96,384]{1,0:T(8,128)} async-done(((f32[768,384]{1,0:T(8,128)}), f32[96,384]{1,0:T(8,128)}) %reduce-scatter.26.cloned.1.call-update) | async-done | bytes 147472
  1370.8 96.4 %reduce-scatter.20.cloned.1.call-done = f32[2,96,3,192]{3,1,2,0:T(8,128)} async-done(((f32[2,768,3,192]{3,1,2,0:T(8,128)}), f32[2,96,3,192]{3,1,2,0:T(8,128)}) %reduce-scatter.20.cloned.1.call-update) | async-done | bytes 442384 | tf_op jit(solution)/shard_map/reduce_scatter | solution.py:56
  1467.3 99.1 %reduce-scatter.22.cloned.1.call-done = f32[2,96,768]{2,1,0:T(8,128)} async-done(((f32[2,768,768]{2,1,0:T(8,128)}), f32[2,96,768]{2,1,0:T(8,128)}) %reduce-scatter.22.cloned.1.call-update) | async-done | bytes 589840 | tf_op jit(solution)/shard_map/reduce_scatter | solution.py:58
  1566.4 99.0 %reduce-scatter.24.cloned.1.call-done = f32[2,768,96]{1,2,0:T(8,128)} async-done(((f32[2,768,768]{1,2,0:T(8,128)}), f32[2,768,96]{1,2,0:T(8,128)}) %reduce-scatter.24.cloned.1.call-update) | async-done | bytes 589840 | tf_op jit(solution)/shard_map/reduce_scatter | solution.py:59
  (746 shorter events, 302.8 us)
Async XLA Ops:
  13.9 61.0 %all-gather.32.cloned.1.call-start = ((), (), s32[]{:S(2)}) async-start(), calls=%async_computation.18 | async-start | bytes 2654208 | tf_op jit(solution)/shard_map/while/body/eval_jaxpr/all_gather | solution.py:44
  14.7 80.6 %all-gather.34.cloned.1.call-start = ((), (), s32[]{:S(2)}) async-start(), calls=%async_computation.19 | async-start | bytes 1966080 | tf_op jit(solution)/shard_map/while/body/eval_jaxpr/all_gather | solution.py:25
  16.5 162.3 %reduce-scatter.34.cloned.1.call-start = ((), (), s32[]{:S(2)}) async-start(), calls=%async_computation.20 | async-start | bytes 3932160 | tf_op jit(solution)/shard_map/while/body/eval_jaxpr/reduce_scatter | solution.py:29
  53.7 46.2 %copy-start.18 = (bf16[1,192,768]{2,1,0:T(8,128)(2,1)}, bf16[1,192,768]{2,1,0:T(8,128)(2,1)S(1)}, u32[]{:S(2)}) copy-start(bf16[1,192,768]{2,1,0:T(8,128)(2,1)S(1)} %copy.265) | copy-start | bytes 884740 | tf_op jit(solution)/shard_map/while
  103.0 92.8 %all-gather.38.cloned.1.call-start = ((), (), s32[]{:S(2)}) async-start(), calls=%async_computation.22 | async-start | bytes 2654208 | tf_op jit(solution)/shard_map/while/body/eval_jaxpr/all_gather | solution.py:46
  103.5 112.5 %all-gather.36.cloned.1.call-start = ((), (), s32[]{:S(2)}) async-start(), calls=%async_computation.21 | async-start | bytes 1966080 | tf_op jit(solution)/shard_map/while/body/eval_jaxpr/all_gather | solution.py:25
  180.1 47.6 %copy-start.44 = (f32[256]{0:T(256)}, f32[256]{0:T(256)S(1)}, u32[]{:S(2)}) copy-start(f32[256]{0:T(256)S(1)} %broadcast_multiply_fusion.8) | copy-start | bytes 3076 | tf_op jit(solution)/shard_map/while
  180.3 47.4 %copy-start.71 = (f32[256]{0:T(256)}, f32[256]{0:T(256)S(1)}, u32[]{:S(2)}) copy-start(f32[256]{0:T(256)S(1)} %multiply_reduce_fusion.24) | copy-start | bytes 3076 | tf_op jit(solution)/shard_map/while
  180.3 47.3 %copy-start.52 = (f32[256]{0:T(256)}, f32[256]{0:T(256)S(1)}, u32[]{:S(2)}) copy-start(f32[256]{0:T(256)S(1)} %fusion.276) | copy-start | bytes 3076 | tf_op jit(solution)/shard_map/while
  181.3 89.1 %all-gather.40.cloned.1.call-start = ((), (), s32[]{:S(2)}) async-start(), calls=%async_computation.23 | async-start | bytes 2654208 | tf_op jit(solution)/shard_map/while/body/eval_jaxpr/all_gather | solution.py:47
  181.9 147.2 %reduce-scatter.36.cloned.1.call-start = ((), (), s32[]{:S(2)}) async-start(), calls=%async_computation.24 | async-start | bytes 3932160 | tf_op jit(solution)/shard_map/while/body/eval_jaxpr/reduce_scatter | solution.py:29
  275.3 179.3 %all-gather.42.cloned.1.call-start = ((), (), s32[]{:S(2)}) async-start(), calls=%async_computation.25 | async-start | bytes 1966080 | tf_op jit(solution)/shard_map/while/body/eval_jaxpr/all_gather | solution.py:33
  304.1 25.0 %copy-start.4 = (f32[256,768]{1,0:T(8,128)}, f32[256,768]{1,0:T(8,128)S(1)}, u32[]{:S(2)}) copy-start(f32[256,768]{1,0:T(8,128)S(1)} %bitcast_convert_fusion.4) | copy-start | bytes 2359300 | tf_op jit(solution)/shard_map/while
  316.4 12.7 copy-start.48
  316.4 12.7 copy-start.53
  330.6 23.0 %copy-start.35 = (f32[768]{0:T(1024)S(1)}, f32[768]{0:T(1024)}, u32[]{:S(2)}) copy-start(f32[768]{0:T(1024)} %get-tuple-element.599) | copy-start | bytes 9220 | tf_op jit(solution)/shard_map/while
  333.1 43.9 %copy-start.33 = (f32[768]{0:T(1024)S(1)}, f32[768]{0:T(1024)}, u32[]{:S(2)}) copy-start(f32[768]{0:T(1024)} %get-tuple-element.606) | copy-start | bytes 9220 | tf_op jit(solution)/shard_map/while
  341.1 47.5 %copy-start.49 = (bf16[8,192]{1,0:T(8,128)(2,1)}, bf16[8,192]{1,0:T(8,128)(2,1)S(1)}, u32[]{:S(2)}) copy-start(bf16[8,192]{1,0:T(8,128)(2,1)S(1)} %convert_element_type.319) | copy-start | bytes 9220 | tf_op jit(solution)/shard_map/while
  354.4 21.7 %copy-start.39 = (f32[2,768]{1,0:T(2,128)}, f32[2,768]{1,0:T(2,128)S(1)}, u32[]{:S(2)}) copy-start(f32[2,768]{1,0:T(2,128)S(1)} %get-tuple-element.602) | copy-start | bytes 18436 | tf_op jit(solution)/shard_map/while
  437.6 55.0 %reduce-scatter.38.cloned.1.call-start = ((), (), s32[]{:S(2)}) async-start(), calls=%async_computation.26 | async-start | bytes 1966080 | tf_op jit(solution)/shard_map/while/body/eval_jaxpr/reduce_scatter | solution.py:37
  461.6 31.0 %copy-start.1 = (f32[256,768]{1,0:T(8,128)S(1)}, f32[256,768]{1,0:T(8,128)}, u32[]{:S(2)}) copy-start(f32[256,768]{1,0:T(8,128)} %copy-done) | copy-start | bytes 2359300 | tf_op jit(solution)/shard_map/while
  461.6 31.0 %copy-start.46 = (f32[256]{0:T(256)S(1)}, f32[256]{0:T(256)}, u32[]{:S(2)}) copy-start(f32[256]{0:T(256)} %copy-done.44) | copy-start | bytes 3076 | tf_op jit(solution)/shard_map/while
  461.6 31.0 %copy-start.54 = (f32[256]{0:T(256)S(1)}, f32[256]{0:T(256)}, u32[]{:S(2)}) copy-start(f32[256]{0:T(256)} %copy-done.52) | copy-start | bytes 3076 | tf_op jit(solution)/shard_map/while
  464.2 29.8 %copy-start.72 = (f32[256]{0:T(256)S(1)}, f32[256]{0:T(256)}, u32[]{:S(2)}) copy-start(f32[256]{0:T(256)} %copy-done.71) | copy-start | bytes 3076 | tf_op jit(solution)/shard_map/while
  464.3 52.9 %all-gather.44.cloned.1.call-start = ((), (), s32[]{:S(2)}) async-start(), calls=%async_computation.27 | async-start | bytes 1966080 | tf_op jit(solution)/shard_map/while/body/eval_jaxpr/all_gather | solution.py:33
  497.3 61.6 %reduce-scatter.40.cloned.1.call-start = ((), (), s32[]{:S(2)}) async-start(), calls=%async_computation.28 | async-start | bytes 1966080 | tf_op jit(solution)/shard_map/while/body/eval_jaxpr/reduce_scatter | solution.py:37
  506.1 13.9 copy-start.81
  545.1 13.8 copy-start.6
  545.1 15.9 copy-start.27
  561.3 58.2 %all-gather.32.cloned.1.call-start = ((), (), s32[]{:S(2)}) async-start(), calls=%async_computation.18 | async-start | bytes 2654208 | tf_op jit(solution)/shard_map/while/body/eval_jaxpr/all_gather | solution.py:44
  561.9 78.0 %all-gather.34.cloned.1.call-start = ((), (), s32[]{:S(2)}) async-start(), calls=%async_computation.19 | async-start | bytes 1966080 | tf_op jit(solution)/shard_map/while/body/eval_jaxpr/all_gather | solution.py:25
  563.8 159.6 %reduce-scatter.34.cloned.1.call-start = ((), (), s32[]{:S(2)}) async-start(), calls=%async_computation.20 | async-start | bytes 3932160 | tf_op jit(solution)/shard_map/while/body/eval_jaxpr/reduce_scatter | solution.py:29
  599.2 45.3 %copy-start.18 = (bf16[1,192,768]{2,1,0:T(8,128)(2,1)}, bf16[1,192,768]{2,1,0:T(8,128)(2,1)S(1)}, u32[]{:S(2)}) copy-start(bf16[1,192,768]{2,1,0:T(8,128)(2,1)S(1)} %copy.265) | copy-start | bytes 884740 | tf_op jit(solution)/shard_map/while
  647.6 92.8 %all-gather.38.cloned.1.call-start = ((), (), s32[]{:S(2)}) async-start(), calls=%async_computation.22 | async-start | bytes 2654208 | tf_op jit(solution)/shard_map/while/body/eval_jaxpr/all_gather | solution.py:46
  648.2 112.5 %all-gather.36.cloned.1.call-start = ((), (), s32[]{:S(2)}) async-start(), calls=%async_computation.21 | async-start | bytes 1966080 | tf_op jit(solution)/shard_map/while/body/eval_jaxpr/all_gather | solution.py:25
  724.7 47.6 %copy-start.44 = (f32[256]{0:T(256)}, f32[256]{0:T(256)S(1)}, u32[]{:S(2)}) copy-start(f32[256]{0:T(256)S(1)} %broadcast_multiply_fusion.8) | copy-start | bytes 3076 | tf_op jit(solution)/shard_map/while
  724.9 47.4 %copy-start.71 = (f32[256]{0:T(256)}, f32[256]{0:T(256)S(1)}, u32[]{:S(2)}) copy-start(f32[256]{0:T(256)S(1)} %multiply_reduce_fusion.24) | copy-start | bytes 3076 | tf_op jit(solution)/shard_map/while
  725.0 47.4 %copy-start.52 = (f32[256]{0:T(256)}, f32[256]{0:T(256)S(1)}, u32[]{:S(2)}) copy-start(f32[256]{0:T(256)S(1)} %fusion.276) | copy-start | bytes 3076 | tf_op jit(solution)/shard_map/while
  726.0 89.1 %all-gather.40.cloned.1.call-start = ((), (), s32[]{:S(2)}) async-start(), calls=%async_computation.23 | async-start | bytes 2654208 | tf_op jit(solution)/shard_map/while/body/eval_jaxpr/all_gather | solution.py:47
  726.6 147.2 %reduce-scatter.36.cloned.1.call-start = ((), (), s32[]{:S(2)}) async-start(), calls=%async_computation.24 | async-start | bytes 3932160 | tf_op jit(solution)/shard_map/while/body/eval_jaxpr/reduce_scatter | solution.py:29
  819.9 179.3 %all-gather.42.cloned.1.call-start = ((), (), s32[]{:S(2)}) async-start(), calls=%async_computation.25 | async-start | bytes 1966080 | tf_op jit(solution)/shard_map/while/body/eval_jaxpr/all_gather | solution.py:33
  848.7 25.0 %copy-start.4 = (f32[256,768]{1,0:T(8,128)}, f32[256,768]{1,0:T(8,128)S(1)}, u32[]{:S(2)}) copy-start(f32[256,768]{1,0:T(8,128)S(1)} %bitcast_convert_fusion.4) | copy-start | bytes 2359300 | tf_op jit(solution)/shard_map/while
  861.0 12.7 copy-start.48
  861.0 12.7 copy-start.53
  875.3 23.0 %copy-start.35 = (f32[768]{0:T(1024)S(1)}, f32[768]{0:T(1024)}, u32[]{:S(2)}) copy-start(f32[768]{0:T(1024)} %get-tuple-element.599) | copy-start | bytes 9220 | tf_op jit(solution)/shard_map/while
  877.8 43.9 %copy-start.33 = (f32[768]{0:T(1024)S(1)}, f32[768]{0:T(1024)}, u32[]{:S(2)}) copy-start(f32[768]{0:T(1024)} %get-tuple-element.606) | copy-start | bytes 9220 | tf_op jit(solution)/shard_map/while
  885.7 47.5 %copy-start.49 = (bf16[8,192]{1,0:T(8,128)(2,1)}, bf16[8,192]{1,0:T(8,128)(2,1)S(1)}, u32[]{:S(2)}) copy-start(bf16[8,192]{1,0:T(8,128)(2,1)S(1)} %convert_element_type.319) | copy-start | bytes 9220 | tf_op jit(solution)/shard_map/while
  899.0 21.7 %copy-start.39 = (f32[2,768]{1,0:T(2,128)}, f32[2,768]{1,0:T(2,128)S(1)}, u32[]{:S(2)}) copy-start(f32[2,768]{1,0:T(2,128)S(1)} %get-tuple-element.602) | copy-start | bytes 18436 | tf_op jit(solution)/shard_map/while
  982.2 55.1 %reduce-scatter.38.cloned.1.call-start = ((), (), s32[]{:S(2)}) async-start(), calls=%async_computation.26 | async-start | bytes 1966080 | tf_op jit(solution)/shard_map/while/body/eval_jaxpr/reduce_scatter | solution.py:37
  1006.3 31.0 %copy-start.1 = (f32[256,768]{1,0:T(8,128)S(1)}, f32[256,768]{1,0:T(8,128)}, u32[]{:S(2)}) copy-start(f32[256,768]{1,0:T(8,128)} %copy-done) | copy-start | bytes 2359300 | tf_op jit(solution)/shard_map/while
  1006.3 31.0 %copy-start.46 = (f32[256]{0:T(256)S(1)}, f32[256]{0:T(256)}, u32[]{:S(2)}) copy-start(f32[256]{0:T(256)} %copy-done.44) | copy-start | bytes 3076 | tf_op jit(solution)/shard_map/while
  1006.3 31.0 %copy-start.54 = (f32[256]{0:T(256)S(1)}, f32[256]{0:T(256)}, u32[]{:S(2)}) copy-start(f32[256]{0:T(256)} %copy-done.52) | copy-start | bytes 3076 | tf_op jit(solution)/shard_map/while
  1008.9 29.8 %copy-start.72 = (f32[256]{0:T(256)S(1)}, f32[256]{0:T(256)}, u32[]{:S(2)}) copy-start(f32[256]{0:T(256)} %copy-done.71) | copy-start | bytes 3076 | tf_op jit(solution)/shard_map/while
  1008.9 53.0 %all-gather.44.cloned.1.call-start = ((), (), s32[]{:S(2)}) async-start(), calls=%async_computation.27 | async-start | bytes 1966080 | tf_op jit(solution)/shard_map/while/body/eval_jaxpr/all_gather | solution.py:33
  1042.0 61.6 %reduce-scatter.40.cloned.1.call-start = ((), (), s32[]{:S(2)}) async-start(), calls=%async_computation.28 | async-start | bytes 1966080 | tf_op jit(solution)/shard_map/while/body/eval_jaxpr/reduce_scatter | solution.py:37
  1050.8 13.9 copy-start.81
  1092.7 12.9 copy-start.27
  1109.6 65.3 %reduce-scatter.28.cloned.1.call-start = ((), (), s32[]{:S(2)}) async-start(), calls=%async_computation.15 | async-start | bytes 442368
  1112.1 126.6 %reduce-scatter.30.cloned.1.call-start = ((), (), s32[]{:S(2)}) async-start(), calls=%async_computation.16 | async-start | bytes 442368
  1113.9 188.5 %reduce-scatter.32.cloned.1.call-start = ((), (), s32[]{:S(2)}) async-start(), calls=%async_computation.17 | async-start | bytes 442368
  1114.9 254.1 %reduce-scatter.26.cloned.1.call-start = ((), (), s32[]{:S(2)}) async-start(), calls=%async_computation.14 | async-start | bytes 1327104
  1118.1 349.2 %reduce-scatter.20.cloned.1.call-start = ((), (), s32[]{:S(2)}) async-start(), calls=%async_computation.11 | async-start | bytes 5308416 | tf_op jit(solution)/shard_map/reduce_scatter | solution.py:56
  1123.7 442.6 %reduce-scatter.22.cloned.1.call-start = ((), (), s32[]{:S(2)}) async-start(), calls=%async_computation.12 | async-start | bytes 5308416 | tf_op jit(solution)/shard_map/reduce_scatter | solution.py:58
  1124.5 540.9 %reduce-scatter.24.cloned.1.call-start = ((), (), s32[]{:S(2)}) async-start(), calls=%async_computation.13 | async-start | bytes 5308416 | tf_op jit(solution)/shard_map/reduce_scatter | solution.py:59
  (142 other events, 524.1 us)
Sparse Core Ops, SparseCore 0:
  16.9 57.9 all-gather.31
  77.1 18.1 all-gather.33
  103.1 37.9 reduce-scatter.33
  143.3 52.3 all-gather.37
  197.8 18.1 all-gather.35
  218.3 52.0 all-gather.39
  275.4 36.4 reduce-scatter.35
  437.7 16.8 all-gather.41
  464.4 28.1 reduce-scatter.37
  497.5 19.6 all-gather.43
  530.7 28.1 reduce-scatter.39
  564.0 55.4 all-gather.31
  621.7 18.1 all-gather.33
  647.7 37.9 reduce-scatter.33
  688.0 52.3 all-gather.37
  742.5 18.1 all-gather.35
  763.0 52.0 all-gather.39
  820.0 36.4 reduce-scatter.35
  982.3 16.8 all-gather.41
  1009.0 28.1 reduce-scatter.37
  1042.1 19.6 all-gather.43
  1075.4 28.1 reduce-scatter.39
Sparse Core Ops, SparseCore 1:
  1113.3 61.5 reduce-scatter.27
  1178.1 60.5 reduce-scatter.29
  1241.8 60.5 reduce-scatter.31
  1305.8 63.1 reduce-scatter.25
  1373.2 94.0 reduce-scatter.19
  1471.5 94.8 reduce-scatter.21
  1570.5 94.8 reduce-scatter.23
where the time goes:
time: 1680 us; the launch traced here: 1670 us
  waiting for transfers between devices  865 us (51%)
  blocking collectives  388 us (23%)
  local copies, waits for them, and re-layouts  172 us (10%)
  matrix products  133 us (8%)
  other arithmetic  89.8 us (5%)
    unnamed x11, waiting for transfers between devices  230 us
    reduce_scatter x1, waiting for transfers between devices, reduce_grads(): lax.psum_scatter(local_grads[2], 'dp', scatter_dimension=1, tiled=True)  99.1 us
    reduce_scatter x1, waiting for transfers between devices, reduce_grads(): lax.psum_scatter(local_grads[3], 'dp', scatter_dimension=2, tiled=True)  99 us
    reduce_scatter x1, waiting for transfers between devices, reduce_grads(): lax.psum_scatter(local_grads[0], 'dp', scatter_dimension=1, tiled=True)  96.4 us
    while x8, blocking collectives  92.6 us
    all_gather x2, waiting for transfers between devices, fetch_weights(): lax.all_gather(shards[3], 'dp', axis=2, tiled=True)  85.5 us
    reduce_scatter x4, waiting for transfers between devices, collect_grads(): lax.psum_scatter(partial_value.astype(jnp.bfloat16), 'tensor', scatter_di...  74.6 us
    all_gather x2, blocking collectives, fetch_weights(): lax.all_gather(shards[1], 'dp', axis=2, tiled=True)  67.6 us
  transfers between devices with their start and end apart: 29, of which 25 were waited for; matrix products, arithmetic and copies ran while one was open for 13% of the time, Pallas kernels for 0%

commit v1 on v0

v1 whole, which is shorter than its diff:
```python
import functools
import math

import jax
import jax.numpy as jnp
from jax import lax
from jax.experimental import pallas as pl
from jax.experimental.pallas import tpu as pltpu
from jax.sharding import PartitionSpec as P

HEAD = 64
SEG = 128
GROUP = 8
F32, BF16 = jnp.float32, jnp.bfloat16
VMEM = pltpu.VMEM
ANY = pl.BlockSpec(memory_space=pl.ANY)
WHOLE = pl.BlockSpec(memory_space=pltpu.VMEM)
SMEM = pl.BlockSpec(memory_space=pltpu.SMEM)
PARAMS = pltpu.CompilerParams(vmem_limit_bytes=60 << 20)
EPS = 1e-05
SCALE = HEAD ** (-0.5)
RSQRT2 = 1.0 / math.sqrt(2.0)
RSQRT2PI = 1.0 / math.sqrt(2.0 * math.pi)


def nn(a, b):
    return lax.dot_general(a, b, (((1,), (0,)), ((), ())), preferred_element_type=F32)


def nt(a, b):
    return lax.dot_general(a, b, (((1,), (1,)), ((), ())), preferred_element_type=F32)


def tn(a, b):
    return lax.dot_general(a, b, (((0,), (0,)), ((), ())), preferred_element_type=F32)


def norm_parts(h):
    center = h - jnp.mean(h, axis=-1, keepdims=True)
    rstd = lax.rsqrt(jnp.mean(center * center, axis=-1, keepdims=True) + EPS)
    return center * rstd, rstd


def norm_back(grad, normed, rstd, gain):
    dn = grad * gain
    return rstd * (
        dn
        - jnp.mean(dn, axis=-1, keepdims=True)
        - normed * jnp.mean(dn * normed, axis=-1, keepdims=True)
    )


def gelu_both(u):
    cdf = 0.5 + 0.5 * lax.erf(u * RSQRT2)
    return u * cdf, cdf + u * (jnp.exp(-0.5 * u * u) * RSQRT2PI)


def halves(pair):
    lane = lax.broadcasted_iota(jnp.int32, pair.shape, 1)
    zero = jnp.zeros_like(pair)
    return jnp.concatenate(
        [jnp.where(lane < HEAD, pair, zero), jnp.where(lane < HEAD, zero, pair)], axis=0
    )


def unhalve(stacked):
    lane = lax.broadcasted_iota(jnp.int32, (SEG, 2 * HEAD), 1)
    return jnp.where(lane < HEAD, stacked[:SEG], stacked[SEG:])


def half_softmax(s):
    top = jnp.concatenate(
        [
            jnp.broadcast_to(jnp.max(s[:, :SEG], axis=-1, keepdims=True), (SEG, SEG)),
            jnp.broadcast_to(jnp.max(s[:, SEG:], axis=-1, keepdims=True), (SEG, SEG)),
        ],
        axis=1,
    )
    ex = jnp.exp(s - top)
    inv = jnp.concatenate(
        [
            jnp.broadcast_to(1.0 / jnp.sum(ex[:, :SEG], axis=-1, keepdims=True), (SEG, SEG)),
            jnp.broadcast_to(1.0 / jnp.sum(ex[:, SEG:], axis=-1, keepdims=True), (SEG, SEG)),
        ],
        axis=1,
    )
    return ex * inv


def call(body, outs, out_specs, in_specs, scratch=(), flops=0, nbytes=0):
    return pl.pallas_call(
        body,
        out_shape=outs,
        in_specs=in_specs,
        out_specs=out_specs,
        scratch_shapes=list(scratch),
        compiler_params=PARAMS,
        cost_estimate=pl.CostEstimate(
            flops=int(flops), bytes_accessed=int(nbytes), transcendentals=0
        ),
    )


def sds(shape, dtype):
    return jax.ShapeDtypeStruct(shape, dtype)


def fetch(plan, pieces, packs, blk_ref, dst, sems):
    by_j = [[], [], [], []]
    n = 0
    for which, lead, j, slot in plan:
        for p in range(packs):
            src = pieces[which]
            if slot is None:
                src, to = src.at[j, p], dst.at[p, j]
            else:
                src = src.at[(*lead, p)]
                rows = src.shape[0]
                to = dst.at[p, j, pl.ds(pl.multiple_of(blk_ref[slot] * rows, 16), rows)]
            copy = pltpu.make_async_copy(src, to, sems.at[n])
            copy.start()
            by_j[j].append(copy)
            n += 1
    return by_j


def n_copies(plan, packs):
    return len(plan) * packs


def attn_forward(plan, n_pieces, blk, x, nv, pieces):
    rows, d = x.shape
    segs, quarter = rows // SEG, d // 4

    def body(blk_ref, x_ref, nv_ref, *refs):
        ins, refs = refs[:n_pieces], refs[n_pieces:]
        (w_out, q_ref, k_ref, v_ref, o_ref, p_ref, xt_ref, y_ref, n_ref, r_ref, yl_ref) = refs[:11]
        raw, w, sems, wsem = refs[11:]
        copies = fetch(plan, ins, 1, blk_ref, raw, sems)
        xt_ref[...] = x_ref[...].T
        for j in range(4):
            for c in copies[j]:
                c.wait()
        for t in range(4):
            for half in range(2):
                a = raw[0, 2 * half, :, t * quarter : (t + 1) * quarter]
                b = raw[0, 2 * half + 1, :, t * quarter : (t + 1) * quarter]
                w[t, :, 2 * half * quarter : 2 * (half + 1) * quarter] = jnp.concatenate(
                    [a, b], axis=1
                )
        save = pltpu.make_async_copy(w, w_out, wsem)
        save.start()
        q_ref[...] = nn(x_ref[...], w[0]).astype(BF16)
        k_ref[...] = nn(x_ref[...], w[1]).astype(BF16)
        v_ref[...] = nn(x_ref[...], w[2]).astype(BF16)

        def seg(t, _):
            at = pl.ds(pl.multiple_of(t * SEG, SEG), SEG)
            for pair in range(d // SEG):
                cols = slice(pair * SEG, (pair + 1) * SEG)
                s = nt(q_ref[at, cols], halves(k_ref[at, cols])) * SCALE
                p = half_softmax(s).astype(BF16)
                p_ref[t, pair] = p
                o_ref[at, cols] = nn(p, halves(v_ref[at, cols])).astype(BF16)
            return 0

        lax.fori_loop(0, segs, seg, 0)
        y_ref[...] = nt(o_ref[...], w[3])

        def ln(t, _):
            at = pl.ds(pl.multiple_of(t * SEG, SEG), SEG)
            n, r = norm_parts(x_ref[at].astype(F32) + y_ref[at])
            y = n * nv_ref[0:1] + nv_ref[4:5]
            y_ref[at] = y
            n_ref[at] = n.astype(BF16)
            r_ref[at] = r
            yl_ref[t] = y[0:8]
            return 0

        lax.fori_loop(0, segs, ln, 0)
        save.wait()

    outs = (
        sds((4, d, d), BF16),
        *(sds((rows, d), BF16) for _ in range(4)),
        sds((segs, d // SEG, SEG, 2 * SEG), BF16),
        sds((d, rows), BF16),
        sds((rows, d), F32),
        sds((rows, d), BF16),
        sds((rows, 1), F32),
        sds((segs, 8, d), F32),
    )
    return call(
        body,
        outs,
        (ANY,) + (WHOLE,) * 10,
        [SMEM, WHOLE, WHOLE] + [ANY] * n_pieces,
        [
            VMEM((1, 4, d, d), BF16),
            VMEM((4, d, d), BF16),
            pltpu.SemaphoreType.DMA((n_copies(plan, 1),)),
            pltpu.SemaphoreType.DMA,
        ],
        flops=2 * rows * d * d * 4,
        nbytes=20e6,
    )(blk, x, nv, *pieces)


def mlp_forward(plan, n_pieces, blk, y, lead_y, cot, nv, pieces):
    rows, d = y.shape
    leads = lead_y.shape[0]
    total = rows + leads
    tile = total if total <= 640 else 512
    assert total % tile == 0

    def body(blk_ref, y_ref, yl_ref, cot_ref, nv_ref, *refs):
        ins, refs = refs[:n_pieces], refs[n_pieces:]
        (w_out, gb_out, gp_out, ybt_ref, dmt_ref, dm_ref, dh_ref, res_ref, sums_ref) = refs[:9]
        zl_ref, nl_ref, rl_ref, ybl_ref = refs[9:13]
        w, yb, m, gb, gp, sems, wsem, gsem = refs[13:]
        copies = fetch(plan, ins, 2, blk_ref, w, sems)
        yb[0:rows] = y_ref[...].astype(BF16)
        yb[rows:total] = yl_ref[...].astype(BF16)
        ybl_ref[...] = yb[rows:total]
        ybt_ref[...] = yb[0:rows].T
        saves = []
        for j in range(4):
            for c in copies[j]:
                c.wait()
            if j >= 2:
                saves[2 * (j - 2)].wait()
                saves[2 * (j - 2) + 1].wait()

            def up(t, _, j=j):
                at = pl.ds(pl.multiple_of(t * tile, 16), tile)
                g, gd = gelu_both(nn(yb[at], w[0, j]))
                gb[j % 2, at] = g.astype(BF16)
                gp[j % 2, at] = gd.astype(BF16)
                part = nt(gb[j % 2, at], w[1, j])
                m[at] = part if j == 0 else m[at] + part
                return 0

            if total == tile:
                up(0, 0)
            else:
                lax.fori_loop(0, total // tile, up, 0)
            for buf, out, at in ((gb, gb_out, 0), (gp, gp_out, 1)):
                saves.append(
                    pltpu.make_async_copy(buf.at[j % 2], out.at[j], gsem.at[2 * j + at])
                )
                saves[-1].start()
        save = pltpu.make_async_copy(w, w_out, wsem)
        save.start()
        gain, bias = nv_ref[1:2], nv_ref[5:6]
        sums_ref[...] = jnp.zeros_like(sums_ref)

        def main(t, _):
            at = pl.ds(pl.multiple_of(t * SEG, SEG), SEG)
            n, r = norm_parts(y_ref[at] + m[at])
            res_ref[at] = (n * gain + bias).astype(BF16)
            row = lax.broadcasted_iota(jnp.int32, (SEG, d), 0)
            grad = jnp.where(row == 0, 0.0, cot_ref[at].astype(F32))
            sums_ref[0:1] += jnp.sum(grad * n, axis=0, keepdims=True)
            sums_ref[1:2] += jnp.sum(grad, axis=0, keepdims=True)
            dh = norm_back(grad, n, r, gain)
            dh_ref[at] = dh
            dm_ref[at] = dh.astype(BF16)
            return 0

        lax.fori_loop(0, rows // SEG, main, 0)

        def lead(t, _):
            at = pl.ds(pl.multiple_of(t * SEG, SEG), SEG)
            n, r = norm_parts(
                yl_ref[at].astype(F32) + m[pl.ds(pl.multiple_of(rows + t * SEG, SEG), SEG)]
            )
            zl_ref[at] = n * gain + bias
            nl_ref[at] = n
            rl_ref[at] = r
            return 0

        lax.fori_loop(0, leads // SEG, lead, 0)
        dmt_ref[...] = dm_ref[...].T
        for s in saves[4:]:
            s.wait()
        save.wait()

    outs = (
        sds((2, 4, d, d), BF16),
        sds((4, total, d), BF16),
        sds((4, total, d), BF16),
        sds((d, rows), BF16),
        sds((d, rows), BF16),
        sds((rows, d), BF16),
        sds((rows, d), F32),
        sds((rows, d), BF16),
        sds((8, d), F32),
        sds((leads, d), F32),
        sds((leads, d), F32),
        sds((leads, 1), F32),
        sds((leads, d), BF16),
    )
    return call(
        body,
        outs,
        (ANY, ANY, ANY) + (WHOLE,) * 10,
        [SMEM] + [WHOLE] * 4 + [ANY] * n_pieces,
        [
            VMEM((2, 4, d, d), BF16),
            VMEM((total, d), BF16),
            VMEM((total, d), F32),
            VMEM((2, total, d), BF16),
            VMEM((2, total, d), BF16),
            pltpu.SemaphoreType.DMA((n_copies(plan, 2),)),
            pltpu.SemaphoreType.DMA,
            pltpu.SemaphoreType.DMA((8,)),
        ],
        flops=2 * total * d * d * 8,
        nbytes=40e6,
    )(blk, y, lead_y, cot, nv, *pieces)


def put_blocks(blocked, blk_ref, src, out, lead, sems, base, slots):
    if not blocked:
        copies = [pltpu.make_async_copy(src, out.at[lead], sems.at[base])]
    else:
        rows = src.shape[0] // slots
        copies = [
            pltpu.make_async_copy(
                src.at[pl.ds(pl.multiple_of(blk_ref[s] * rows, 16), rows)],
                out.at[(lead[0], s, lead[1], pl.ds(0, rows))],
                sems.at[base + s],
            )
            for s in range(slots)
        ]
    for c in copies:
        c.start()
    return copies


def mlp_backward(core, slots, blocked, blk, dm, dmt, ybt, gb, gp, w, start):
    rows, d = dm.shape
    dblk = d // slots
    per = slots if blocked else 1

    def body(blk_ref, dm_ref, dmt_ref, ybt_ref, gb_hbm, gp_hbm, w_hbm, start_ref, g_out, dy_ref, *scr):
        gb_s, gp_s, w_s, du_s, gr, sin, sout = scr
        loads = []
        for y in range(2):
            j = 2 * core + y
            pair = [
                (gb_hbm.at[j, pl.ds(0, rows)], gb_s.at[y]),
                (gp_hbm.at[j, pl.ds(0, rows)], gp_s.at[y]),
                (w_hbm.at[1, j], w_s.at[y, 1]),
                (w_hbm.at[0, j], w_s.at[y, 0]),
            ]
            loads.append(
                [pltpu.make_async_copy(a, b, sin.at[4 * y + i]) for i, (a, b) in enumerate(pair)]
            )
            for c in loads[-1]:
                c.start()
        outs = []
        for y in range(2):
            for c in loads[y]:
                c.wait()
            dg = nn(dm_ref[...], w_s[y, 1])
            du_s[...] = (dg * gp_s[y].astype(F32)).astype(BF16)
            gr[y, 1] = nn(dmt_ref[...], gb_s[y]).astype(BF16)
            outs += put_blocks(
                blocked, blk_ref, gr.at[y, 1], g_out, (y, 1), sout, (2 * y) * per, slots
            )
            gr[y, 0] = nn(ybt_ref[...], du_s[...]).astype(BF16)
            outs += put_blocks(
                blocked, blk_ref, gr.at[y, 0], g_out, (y, 0), sout, (2 * y + 1) * per, slots
            )
            part = nt(du_s[...], w_s[y, 0])
            dy_ref[...] = (start_ref[...] if y == 0 else dy_ref[...]) + part
        for c in outs:
            c.wait()

    g_shape = (2, slots, 2, dblk, d) if blocked else (2, 2, d, d)
    return call(
        body,
        (sds(g_shape, BF16), sds((rows, d), F32)),
        (ANY, WHOLE),
        [SMEM, WHOLE, WHOLE, WHOLE, ANY, ANY, ANY, WHOLE],
        [
            VMEM((2, rows, d), BF16),
            VMEM((2, rows, d), BF16),
            VMEM((2, 2, d, d), BF16),
            VMEM((rows, d), BF16),
            VMEM((2, 2, d, d), BF16),
            pltpu.SemaphoreType.DMA((8,)),
            pltpu.SemaphoreType.DMA((4 * per,)),
        ],
        flops=2 * rows * d * d * 8,
        nbytes=20e6,
    )(blk, dm, dmt, ybt, gb, gp, w, start)


def attn_norm_back(dy, lead_dy, n1, r1, nv, sums2):
    rows, d = dy.shape

    def body(dy_ref, ld_ref, n_ref, r_ref, nv_ref, s2_ref, dh_ref, da_ref, dat_ref, sums_ref):
        sums_ref[0:2] = jnp.zeros((2, d), F32)
        sums_ref[2:4] = s2_ref[0:2]
        sums_ref[4:8] = jnp.zeros((4, d), F32)

        def one(t, _):
            at = pl.ds(pl.multiple_of(t * SEG, SEG), SEG)
            row = lax.broadcasted_iota(jnp.int32, (SEG, d), 0)
            grad = dy_ref[at] + jnp.where(row == 0, ld_ref[t][0:1], 0.0)
            n = n_ref[at].astype(F32)
            sums_ref[0:1] += jnp.sum(grad * n, axis=0, keepdims=True)
            sums_ref[1:2] += jnp.sum(grad, axis=0, keepdims=True)
            dh = norm_back(grad, n, r_ref[at], nv_ref[0:1])
            dh_ref[at] = dh
            da_ref[at] = dh.astype(BF16)
            return 0

        lax.fori_loop(0, rows // SEG, one, 0)
        dat_ref[...] = da_ref[...].T

    return call(
        body,
        (sds((rows, d), F32), sds((rows, d), BF16), sds((d, rows), BF16), sds((8, d), F32)),
        (WHOLE,) * 4,
        [WHOLE] * 6,
        flops=rows * d * 20,
        nbytes=8e6,
    )(dy, lead_dy, n1, r1, nv, sums2)


def attn_backward(core, slots, blocked, blk, da, dat, xt, q, k, v, o, p, w, start, sums):
    rows, d = da.shape
    segs, half, quarter = rows // SEG, d // 2, d // 4
    dblk = d // slots
    per = slots if blocked else 1
    pairs = half // SEG

    def body(blk_ref, da_ref, dat_ref, xt_ref, q_ref, k_ref, v_ref, o_ref, p_ref, w_hbm, start_ref,
             sums_ref, g_out, dx_ref, *scr):
        w_s, do_s, dq_s, dk_s, dv_s, gf, gr, ex, sin, sout = scr
        load = pltpu.make_async_copy(w_hbm, w_s, sin)
        load.start()
        if blocked:
            for b in range(slots):
                piece = sums_ref[:, b * dblk : (b + 1) * dblk]
                ex[b] = jnp.zeros((16, d), BF16)
                ex[b, 0:8, 0:dblk] = piece.astype(BF16)
        load.wait()
        cols = slice(core * half, (core + 1) * half)
        do_s[...] = nn(da_ref[...], w_s[3, :, cols]).astype(BF16)
        gf[3] = nn(dat_ref[...], o_ref[:, cols]).astype(BF16)

        def seg(t, _):
            at = pl.ds(pl.multiple_of(t * SEG, SEG), SEG)
            for pair in range(pairs):
                mine = slice(pair * SEG, (pair + 1) * SEG)
                wide = slice(core * half + pair * SEG, core * half + (pair + 1) * SEG)
                dout = do_s[at, mine]
                prob = p_ref[t, core * pairs + pair]
                pf = prob.astype(F32)
                dp = nt(dout, halves(v_ref[at, wide]))
                pd = pf * dp
                total = jnp.concatenate(
                    [
                        jnp.broadcast_to(jnp.sum(pd[:, :SEG], axis=-1, keepdims=True), (SEG, SEG)),
                        jnp.broadcast_to(jnp.sum(pd[:, SEG:], axis=-1, keepdims=True), (SEG, SEG)),
                    ],
                    axis=1,
                )
                ds = (pd - pf * total).astype(BF16)
                dv_s[at, mine] = unhalve(tn(prob, dout)).astype(BF16)
                dq_s[at, mine] = (nn(ds, halves(k_ref[at, wide])) * SCALE).astype(BF16)
                dk_s[at, mine] = (unhalve(tn(ds, q_ref[at, wide])) * SCALE).astype(BF16)
            return 0

        lax.fori_loop(0, segs, seg, 0)
        for t, s in enumerate((dq_s, dk_s, dv_s)):
            gf[t] = nn(xt_ref[...], s[...]).astype(BF16)
        outs = []
        for y in range(2):
            for t in range(4):
                gr[y, :, t * quarter : (t + 1) * quarter] = gf[t, :, y * quarter : (y + 1) * quarter]
            outs += put_blocks(blocked, blk_ref, gr.at[y], g_out, (y, 0), sout, y * per, slots)
            if blocked:
                for s in range(slots):
                    c = pltpu.make_async_copy(
                        ex.at[blk_ref[s]],
                        g_out.at[y, s, 0, pl.ds(dblk, 16)],
                        sout.at[2 * per + y * slots + s],
                    )
                    c.start()
                    outs.append(c)
        dx_ref[...] = (
            start_ref[...]
            + nt(dq_s[...], w_s[0, :, cols])
            + nt(dk_s[...], w_s[1, :, cols])
            + nt(dv_s[...], w_s[2, :, cols])
        )
        for c in outs:
            c.wait()

    g_shape = (2, slots, 1, dblk + 16, d) if blocked else (2, 1, d, d)
    return call(
        body,
        (sds(g_shape, BF16), sds((rows, d), F32)),
        (ANY, WHOLE),
        [SMEM] + [WHOLE] * 8 + [ANY, WHOLE, WHOLE],
        [
            VMEM((4, d, d), BF16),
            *(VMEM((rows, half), BF16) for _ in range(4)),
            VMEM((4, d, half), BF16),
            VMEM((2, d, d), BF16),
            VMEM((slots if blocked else 1, 16, d), BF16),
            pltpu.SemaphoreType.DMA,
            pltpu.SemaphoreType.DMA((4 * per,)),
        ],
        flops=2 * rows * d * half * 8,
        nbytes=20e6,
    )(blk, da, dat, xt, q, k, v, o, p, w, start, sums)


def group_mask():
    a = lax.broadcasted_iota(jnp.int32, (SEG, SEG), 0) // GROUP
    b = lax.broadcasted_iota(jnp.int32, (SEG, SEG), 1) // GROUP
    return a == b


def cross_attn(zl, onehot, nv, w):
    rows, d = zl.shape
    quarter = d // 4
    heads = quarter // HEAD
    tiles = rows // SEG

    def body(z_ref, oh_ref, nv_ref, w_ref, c_ref, qkv_ref, o_ref, p_ref, a_ref):
        def one(t, _):
            at = pl.ds(pl.multiple_of(t * SEG, SEG), SEG)
            c = z_ref[at]
            for i in range(8):
                c += oh_ref[at, i : i + 1].astype(F32) * nv_ref[8 + i : 9 + i]
            c_ref[at] = c
            qkv = nn(c.astype(BF16), w_ref[:, : 3 * quarter]).astype(BF16)
            qkv_ref[at] = qkv
            mask = group_mask()
            os = []
            for h in range(heads):
                q, k, v = (
                    qkv[:, i * quarter + h * HEAD : i * quarter + (h + 1) * HEAD] for i in range(3)
                )
                s = jnp.where(mask, nt(q, k) * SCALE, -1e30)
                ex = jnp.exp(s - jnp.max(s, axis=-1, keepdims=True))
                p = (ex / jnp.sum(ex, axis=-1, keepdims=True)).astype(BF16)
                p_ref[t, h] = p
                os.append(nn(p, v).astype(BF16))
            o = jnp.concatenate(os, axis=1)
            o_ref[at] = o
            a_ref[at] = nt(o, w_ref[:, 3 * quarter :]).astype(BF16)
            return 0

        lax.fori_loop(0, tiles, one, 0)

    return call(
        body,
        (
            sds((rows, d), F32),
            sds((rows, 3 * quarter), BF16),
            sds((rows, quarter), BF16),
            sds((tiles, heads, SEG, SEG), BF16),
            sds((rows, d), BF16),
        ),
        (WHOLE,) * 5,
        [WHOLE] * 4,
        flops=2 * rows * d * d,
        nbytes=3e6,
    )(zl, onehot, nv, w)


def cross_mlp(c, a0, a1, nv, w):
    rows, d = c.shape

    def body(c_ref, a0_ref, a1_ref, nv_ref, w_ref, y_ref, n_ref, r_ref, gb_ref, gp_ref, m_ref):
        n, r = norm_parts(c_ref[...] + (a0_ref[...].astype(F32) + a1_ref[...].astype(F32)))
        n_ref[...] = n
        r_ref[...] = r
        y = n * nv_ref[2:3] + nv_ref[6:7]
        y_ref[...] = y
        g, gd = gelu_both(nn(y.astype(BF16), w_ref[0]))
        gb_ref[...] = g.astype(BF16)
        gp_ref[...] = gd.astype(BF16)
        m_ref[...] = nt(gb_ref[...], w_ref[1]).astype(BF16)

    return call(
        body,
        (
            sds((rows, d), F32),
            sds((rows, d), F32),
            sds((rows, 1), F32),
            sds((rows, d), BF16),
            sds((rows, d), BF16),
            sds((rows, d), BF16),
        ),
        (WHOLE,) * 6,
        [WHOLE] * 5,
        flops=4 * rows * d * d,
        nbytes=5e6,
    )(c, a0, a1, nv, w)


def cross_mlp_back(y, m0, m1, cot, nv, w, gb, gp):
    rows, d = y.shape

    def body(y_ref, m0_ref, m1_ref, cot_ref, nv_ref, w_ref, gb_ref, gp_ref,
             e_ref, dh_ref, gd_ref, gu_ref, dy_ref, sums_ref):
        gain = nv_ref[3:4]
        n, r = norm_parts(y_ref[...] + (m0_ref[...].astype(F32) + m1_ref[...].astype(F32)))
        e_ref[...] = (n * gain + nv_ref[7:8]).astype(BF16)
        grad = cot_ref[...].astype(F32)
        sums_ref[...] = jnp.concatenate(
            [
                jnp.sum(grad * n, axis=0, keepdims=True),
                jnp.sum(grad, axis=0, keepdims=True),
                jnp.zeros((6, d), F32),
            ],
            axis=0,
        )
        dh = norm_back(grad, n, r, gain)
        dh_ref[...] = dh
        dm = dh.astype(BF16)
        du = (nn(dm, w_ref[1]) * gp_ref[...].astype(F32)).astype(BF16)
        dy_ref[...] = nt(du, w_ref[0]).astype(BF16)
        gd_ref[...] = tn(dm, gb_ref[...])
        gu_ref[...] = tn(y_ref[...].astype(BF16), du)

    return call(
        body,
        (
            sds((rows, d), BF16),
            sds((rows, d), F32),
            sds((d, d), F32),
            sds((d, d), F32),
            sds((rows, d), BF16),
            sds((8, d), F32),
        ),
        (WHOLE,) * 6,
        [WHOLE] * 8,
        flops=8 * rows * d * d,
        nbytes=9e6,
    )(y, m0, m1, cot, nv, w, gb, gp)


def cross_attn_back(dh2, d0, d1, n1, r1, c, qkv, o, p, nv, w):
    rows, d = dh2.shape
    quarter = d // 4
    heads = quarter // HEAD
    tiles = rows // SEG

    def body(dh2_ref, d0_ref, d1_ref, n_ref, r_ref, c_ref, qkv_ref, o_ref, p_ref, nv_ref, w_ref,
             dh_ref, dx_ref, g_ref, sums_ref, da_s, dqkv_s):
        grad = dh2_ref[...] + (d0_ref[...].astype(F32) + d1_ref[...].astype(F32))
        n = n_ref[...]
        sums_ref[...] = jnp.concatenate(
            [
                jnp.sum(grad * n, axis=0, keepdims=True),
                jnp.sum(grad, axis=0, keepdims=True),
                jnp.zeros((6, d), F32),
            ],
            axis=0,
        )
        dh = norm_back(grad, n, r_ref[...], nv_ref[2:3])
        dh_ref[...] = dh
        da_s[...] = dh.astype(BF16)
        g_ref[:, 3 * quarter :] = tn(da_s[...], o_ref[...])

        def one(t, _):
            at = pl.ds(pl.multiple_of(t * SEG, SEG), SEG)
            do = nn(da_s[at], w_ref[:, 3 * quarter :]).astype(BF16)
            qkv = qkv_ref[at]
            dq, dk, dv = [], [], []
            for h in range(heads):
                q, k, v = (
                    qkv[:, i * quarter + h * HEAD : i * quarter + (h + 1) * HEAD] for i in range(3)
                )
                doh = do[:, h * HEAD : (h + 1) * HEAD]
                prob = p_ref[t, h]
                pf = prob.astype(F32)
                pd = pf * nt(doh, v)
                ds = (pd - pf * jnp.sum(pd, axis=-1, keepdims=True)).astype(BF16)
                dv.append(tn(prob, doh).astype(BF16))
                dq.append((nn(ds, k) * SCALE).astype(BF16))
                dk.append((tn(ds, q) * SCALE).astype(BF16))
            dqkv_s[at] = jnp.concatenate(dq + dk + dv, axis=1)
            return 0

        lax.fori_loop(0, tiles, one, 0)
        dx_ref[...] = nt(dqkv_s[...], w_ref[:, : 3 * quarter]).astype(BF16)
        g_ref[:, : 3 * quarter] = tn(c_ref[...].astype(BF16), dqkv_s[...])

    return call(
        body,
        (sds((rows, d), F32), sds((rows, d), BF16), sds((d, d), F32), sds((8, d), F32)),
        (WHOLE,) * 4,
        [WHOLE] * 11,
        [VMEM((rows, d), BF16), VMEM((rows, 3 * quarter), BF16)],
        flops=4 * rows * d * d,
        nbytes=6e6,
    )(dh2, d0, d1, n1, r1, c, qkv, o, p, nv, w)


def lead_backward(dh, d0, d1, onehot, nl, rl, ybl, nv, gb, gp, w, main_rows):
    rows, d = dh.shape

    def body(dh_ref, d0_ref, d1_ref, oh_ref, n_ref, r_ref, yb_ref, nv_ref, gb_hbm, gp_hbm, w_hbm,
             dy_ref, gd_ref, gu_ref, sums_ref, gb_s, gp_s, w_s, dm_s, sin):
        loads = []
        for j in range(4):
            pair = [
                (gp_hbm.at[j, pl.ds(main_rows, rows)], gp_s.at[j]),
                (w_hbm.at[1, j], w_s.at[1, j]),
                (w_hbm.at[0, j], w_s.at[0, j]),
            ]
            loads.append(
                [pltpu.make_async_copy(a, b, sin.at[3 * j + i]) for i, (a, b) in enumerate(pair)]
            )
            for c in loads[-1]:
                c.start()
        load0 = pltpu.make_async_copy(gb_hbm.at[0, pl.ds(main_rows, rows)], gb_s, sin.at[12])
        load0.start()
        grad = dh_ref[...] + (d0_ref[...].astype(F32) + d1_ref[...].astype(F32))
        n = n_ref[...]
        tops = [jnp.sum(grad * n, axis=0, keepdims=True), jnp.sum(grad, axis=0, keepdims=True)]
        tops.append(jnp.zeros((6, d), F32))
        for i in range(8):
            tops.append(jnp.sum(oh_ref[:, i : i + 1].astype(F32) * grad, axis=0, keepdims=True))
        sums_ref[...] = jnp.concatenate(tops, axis=0)
        dy = norm_back(grad, n, r_ref[...], nv_ref[1:2])
        dy_ref[...] = dy
        dm_s[...] = dy.astype(BF16)
        load0.wait()
        gd_ref[...] = tn(dm_s[...], gb_s[...])
        for j in range(4):
            for c in loads[j]:
                c.wait()
            du = (nn(dm_s[...], w_s[1, j]) * gp_s[j].astype(F32)).astype(BF16)
            if j == 0:
                gu_ref[...] = tn(yb_ref[...], du)
            dy_ref[...] += nt(du, w_s[0, j])

    return call(
        body,
        (sds((rows, d), F32), sds((d, d), F32), sds((d, d), F32), sds((16, d), F32)),
        (WHOLE,) * 4,
        [WHOLE] * 8 + [ANY] * 3,
        [
            VMEM((rows, d), BF16),
            VMEM((4, rows, d), BF16),
            VMEM((2, 4, d, d), BF16),
            VMEM((rows, d), BF16),
            pltpu.SemaphoreType.DMA((13,)),
        ],
        flops=2 * rows * d * d * 10,
        nbytes=14e6,
    )(dh, d0, d1, onehot, nl, rl, ybl, nv, gb, gp, w)


def swap(axis, size, bit, value):
    return lax.ppermute(value, axis, [(i, i ^ bit) for i in range(size)])


core_swap = functools.partial(swap, "tensor", 4, 1)
y_swap = functools.partial(swap, "tensor", 4, 2)
x_swap = functools.partial(swap, "dp", 8, 1)


def z_swap(k, value):
    return swap("dp", 8, 2 * k, value)


def tied(*trees):
    return lax.optimization_barrier(trees)


PIECES = (
    [(0, (), 0, 0, 0)]
    + [(1, (k - 1,), 0, 0, k) for k in (1, 2, 3)]
    + [(2, (), 0, 1, 0), (3, (), 1, 0, 0)]
    + [(4, (k - 1,), 0, 1, k) for k in (1, 2, 3)]
    + [(5, (k - 1,), 1, 0, k) for k in (1, 2, 3)]
    + [(6, (k,), 1, 1, k) for k in (0, 1)]
    + [(7, (k - 2,), 1, 1, k) for k in (2, 3)]
)
FAST_PLAN = [
    (8 * c + which, lead, 2 * c + y, 4 * x + z)
    for c in range(2)
    for which, lead, y, x, z in PIECES
]
PLAIN_PLAN = [(0, (), j, None) for j in range(4)]


def xor_order(stacked, index, bits):
    shape = stacked.shape
    out = stacked.reshape((2,) * bits + shape[1:])
    for b in range(bits):
        out = jnp.where((index >> (bits - 1 - b)) & 1 == 1, jnp.flip(out, b), out)
    return out.reshape(shape)


def add(*parts):
    total = parts[0].astype(F32)
    for p in parts[1:]:
        total = total + p.astype(F32)
    return total


def low_add(*parts):
    return add(*parts).astype(BF16)


def scatter_sum(g0, g1):
    other = core_swap(g1)

    def own(y, x, zs):
        return (g0[y, x, zs], other[y, x, zs])

    lo, hi = slice(0, 2), slice(2, 4)
    from_x = x_swap(low_add(*own(1, 1, lo)))
    from_y = y_swap(low_add(*own(1, 1, hi)))
    to_x = jnp.concatenate([low_add(*own(0, 1, lo)), low_add(*own(0, 1, hi), from_y)])
    to_y = jnp.concatenate([low_add(*own(1, 0, lo), from_x), low_add(*own(1, 0, hi))])
    from_x, from_y = x_swap(to_x), y_swap(to_y)
    total = add(*own(0, 0, 0), from_x[0], from_y[0])
    back = [
        z_swap(k, low_add(*own(0, 0, k), from_x[k], from_y[k])) for k in (1, 2, 3)
    ]
    return add(total, *back)


def body(tokens, w_qkv, w_out, w_up, w_down, norm_gain, norm_bias, seg_table, seg_ids, cotangent):
    nd, ntens = lax.axis_size("dp"), lax.axis_size("tensor")
    fast = nd == 8
    di, ti = lax.axis_index("dp"), lax.axis_index("tensor")
    seqs, toks, d = tokens.shape
    rows, dblk = seqs * toks, tokens.shape[2] // nd
    per_dev = toks // SEG
    x = tokens.reshape(rows, d)
    cot = cotangent.reshape(rows, d)

    def pack(b):
        return (
            jnp.concatenate([w_qkv[b].reshape(dblk, -1), w_out[b].T], axis=1),
            jnp.stack([w_up[b], w_down[b].T]),
        )

    attn0, mlp0 = pack(0)
    attn1, mlp1 = pack(1)
    small = jnp.concatenate(
        [norm_gain.reshape(4, dblk), norm_bias.reshape(4, dblk), seg_table], axis=0
    )
    onehot = (seg_ids.reshape(-1, 1) == jnp.arange(128, dtype=jnp.int32)).astype(BF16)

    w1 = lax.all_gather(jnp.concatenate([attn1[None], mlp1]), "dp", axis=0)
    w1 = w1.transpose(1, 0, 2, 3).reshape(3, d, d)

    if fast:
        zi, xi = di // 2, di % 2
        blk = jnp.stack([(zi ^ k) * 2 + (xi ^ l) for l in range(2) for k in range(4)]).astype(jnp.int32)
        p1, p2 = attn0[None], mlp0
        sm = jnp.stack([small, x_swap(small)])
        z1 = [z_swap(k, p1) for k in (1, 2, 3)]
        x1, y1 = x_swap(p1), y_swap(p1)
        sz = [z_swap(k, sm) for k in (1, 2, 3)]
        z1, x1, y1, p2, sz = tied(z1, x1, y1, p2, sz)
        c1 = jnp.stack(z1)
        xc1, yc1 = x_swap(c1), y_swap(c1)
        z2 = [z_swap(k, p2) for k in (1, 2, 3)]
        x2, y2 = x_swap(p2), y_swap(p2)
        z2, xc1, yc1, x2, y2 = tied(z2, xc1, yc1, x2, y2)
        c2 = jnp.stack(z2)
        ex1, ey1 = x_swap(jnp.stack([y1, yc1[0]])), y_swap(xc1[1:])
        xc2, yc2 = x_swap(c2), y_swap(c2)
        ex1, ey1, xc2, yc2 = tied(ex1, ey1, xc2, yc2)
        mine1 = [p1, c1, x1, y1, xc1, yc1, ex1, ey1]
        attn_pieces = mine1 + [core_swap(v) for v in mine1]
        ex2, ey2 = x_swap(jnp.stack([y2, yc2[0]])), y_swap(xc2[1:])
        mine2 = [p2, c2, x2, y2, xc2, yc2, ex2, ey2]
        mlp_pieces = mine2 + [core_swap(v) for v in mine2]
        plan = FAST_PLAN
        slots = xor_order(jnp.stack([sm] + sz).reshape(nd, 16, dblk), di, 3)
        nv = slots.transpose(1, 0, 2).reshape(16, d).astype(F32)
    else:
        blk = jnp.zeros((8,), jnp.int32)

        def whole(p):
            g = lax.all_gather(p, ("tensor", "dp"), axis=0)
            g = g.reshape(ntens, nd, p.shape[0], dblk, d).transpose(0, 2, 1, 3, 4)
            g = g.reshape(ntens, p.shape[0], d, d)
            return xor_order(g, ti, 2)

        attn_pieces, mlp_pieces = [whole(attn0[None])], [whole(mlp0)]
        plan = PLAIN_PLAN
        nv = lax.all_gather(small, "dp", axis=1, tiled=True).astype(F32)
    npc = len(attn_pieces)

    w_a, q, k, v, o, p, xt, y, n1, r1, y_first = attn_forward(
        plan, npc, blk, x, nv, attn_pieces
    )

    leaders = jnp.concatenate(
        [
            y_first[:, 0].astype(BF16),
            cot.reshape(-1, SEG, d)[:, 0],
            onehot,
        ],
        axis=1,
    ).reshape(seqs, per_dev, -1)
    width = leaders.shape[-1]
    pay = lax.dynamic_update_slice(
        jnp.zeros((seqs, per_dev * ntens, width), BF16), leaders, (0, per_dev * ti, 0)
    )
    if fast:
        pay = pay + core_swap(pay)
        pay = pay + y_swap(pay)
        pay = jnp.stack([pay, x_swap(pay)])
        pay = jnp.stack([pay] + [z_swap(kk, pay) for kk in (1, 2, 3)])
        first = 0
    else:
        pay = lax.all_gather(lax.psum(pay, "tensor"), "dp", axis=0)
        first = di * seqs * per_dev * ntens
    pay = pay.reshape(-1, width)
    lead_y, lead_cot, lead_hot = pay[:, :d], pay[:, d : 2 * d], pay[:, 2 * d :]

    (w_m, gb, gp, ybt, dmt, dm, dh2, result, sums2, zl, nl, rl, ybl) = mlp_forward(
        plan, npc, blk, y, lead_y, cot, nv, mlp_pieces
    )

    g1, dy = mlp_backward(1, nd, fast, blk, dm, dmt, ybt, gb, gp, w_m, dh2)
    g0, dy = mlp_backward(0, nd, fast, blk, dm, dmt, ybt, gb, gp, w_m, dy)

    def partial_sum(part):
        if fast:
            half = low_add(part, core_swap(part))
            return half, y_swap(half)
        return lax.psum(part.astype(F32), "tensor"), jnp.zeros_like(part)

    c, cqkv, co, cp, ca = cross_attn(zl, lead_hot, nv, w1[0])
    cy, cn, cr, cgb, cgp, cm = cross_mlp(c, *partial_sum(ca), nv, w1[1:])
    e, cdh2, cgd, cgu, cdy, csum2 = cross_mlp_back(
        cy, *partial_sum(cm), lead_cot, nv, w1[1:], cgb, cgp
    )
    cdh, cdx, cga, csum1 = cross_attn_back(
        cdh2, *partial_sum(cdy), cn, cr, c, cqkv, co, cp, nv, w1[0]
    )
    dyl, lgd, lgu, lsum = lead_backward(
        cdh, *partial_sum(cdx), lead_hot, nl, rl, ybl, nv, gb, gp, w_m, rows
    )

    def own_leaders(full):
        part = lax.dynamic_slice_in_dim(full, first, seqs * per_dev * ntens, 0)
        part = part.reshape(seqs, per_dev * ntens, d)
        return lax.dynamic_slice_in_dim(part, per_dev * ti, per_dev, 1).reshape(-1, d)

    lead_dy = jnp.broadcast_to(own_leaders(dyl)[:, None], (rows // SEG, 8, d))
    dh, da, dat, sums = attn_norm_back(dy, lead_dy, n1, r1, nv, sums2)
    a1, dx = attn_backward(1, nd, fast, blk, da, dat, xt, q, k, v, o, p, w_a, dh, sums)
    a0, dx = attn_backward(0, nd, fast, blk, da, dat, xt, q, k, v, o, p, w_a, dx, sums)

    if fast:
        shape = (2, 2, 4)
        gm = scatter_sum(g0.reshape(*shape, *g0.shape[2:]), g1.reshape(*shape, *g1.shape[2:]))
        ga = scatter_sum(a0.reshape(*shape, *a0.shape[2:]), a1.reshape(*shape, *a1.shape[2:]))[0]
        norm_sums = ga[dblk : dblk + 8, :dblk]
        ga = ga[:dblk]
    else:

        def owned(lo, hi):
            g = jnp.concatenate([lo, hi])
            g = xor_order(g, ti, 2).astype(F32)
            g = lax.psum_scatter(g, "tensor", scatter_dimension=0)
            return lax.psum_scatter(g, "dp", scatter_dimension=1, tiled=True)

        gm, ga = owned(g0, g1), owned(a0, a1)[0]
        norm_sums = lax.psum_scatter(
            lax.psum(sums, "tensor"), "dp", scatter_dimension=1, tiled=True
        )

    def rows_of(full):
        return lax.dynamic_slice_in_dim(full, di * dblk, dblk, 0)

    def cols_of(full):
        return lax.dynamic_slice_in_dim(full, di * dblk, dblk, 1)

    gu0, gd0 = gm[0] + rows_of(lgu), gm[1] + rows_of(lgd)
    ga1, gu1, gd1 = rows_of(cga), rows_of(cgu), rows_of(cgd)
    wide = w_qkv.shape[3] * 3
    grad_qkv = jnp.stack([ga[:, :wide], ga1[:, :wide]]).reshape(w_qkv.shape)
    grad_out = jnp.stack([ga[:, wide:].T, ga1[:, wide:].T])
    grad_up = jnp.stack([gu0, gu1])
    grad_down = jnp.stack([gd0.T, gd1.T])
    lsum, csum1, csum2 = cols_of(lsum), cols_of(csum1), cols_of(csum2)
    grad_gain = jnp.stack(
        [
            jnp.stack([norm_sums[0], norm_sums[2] + lsum[0]]),
            jnp.stack([csum1[0], csum2[0]]),
        ]
    )
    grad_bias = jnp.stack(
        [
            jnp.stack([norm_sums[1], norm_sums[3] + lsum[1]]),
            jnp.stack([csum1[1], csum2[1]]),
        ]
    )
    result = result.reshape(-1, SEG, d).at[:, 0].set(own_leaders(e)).reshape(tokens.shape)
    return (
        result,
        dx.reshape(tokens.shape),
        grad_qkv,
        grad_out,
        grad_up,
        grad_down,
        grad_gain,
        grad_bias,
        lsum[8:16],
    )


def solution(mesh):
    return jax.shard_map(
        body,
        mesh=mesh,
        in_specs=(
            P("dp", "tensor", None),
            P(None, "dp", None, "tensor"),
            P(None, "tensor", "dp"),
            P(None, "dp", "tensor"),
            P(None, "tensor", "dp"),
            P(None, None, "dp"),
            P(None, None, "dp"),
            P(None, "dp"),
            P("dp", "tensor"),
            P("dp", "tensor", None),
        ),
        out_specs=(
            P("dp", "tensor", None),
            P("dp", "tensor", None),
            P(None, "dp", None, "tensor"),
            P(None, "tensor", "dp"),
            P(None, "dp", "tensor"),
            P(None, "tensor", "dp"),
            P(None, None, "dp"),
            P(None, None, "dp"),
            P(None, "dp"),
        ),
        check_vma=False,
    )
```

time: 1680 us -> 419 us (0.25)
  waiting for transfers between devices: 865 us -> 136 us
  blocking collectives: 388 us -> 0 us
  local copies, waits for them, and re-layouts: 172 us -> 36.5 us
  matrix products: 133 us -> 0 us
  Pallas kernels: 0 us -> 121 us
  starting transfers between devices: 1.21 us -> 70.3 us
  other arithmetic: 89.8 us -> 34.6 us
    reduce_scatter x11 -> x0, waiting for transfers between devices: 369 us -> none  [the longest x1 99.1 us: reduce_grads(): lax.psum_scatter(local_grads[2], 'dp', scatter_dimension=1, tiled=True)]
    all_gather x16 -> x0, blocking collectives: 289 us -> none  [the longest x2 67.6 us: fetch_weights(): lax.all_gather(shards[1], 'dp', axis=2, tiled=True)]
    all_gather x14 -> x1, waiting for transfers between devices: 262 us -> 0.01 us  [body(): w1 = lax.all_gather(jnp.concatenate([attn1[None], mlp1]), 'dp', axis=0)]
    unnamed x11 -> x1, waiting for transfers between devices: 230 us -> 0.02 us
    ppermute x0 -> x68, waiting for transfers between devices: none -> 136 us  [swap(): return lax.ppermute(value, axis, [(i, i ^ bit) for i in range(size)])]
    dot_general x72 -> x0, matrix products: 126 us -> none  [the longest x4 26.3 us: block_forward(): upward = jnp.dot(normed_sent, w_up, preferred_element_type=jnp.float32)]
    pallas_call x0 -> x12, Pallas kernels: none -> 121 us  [the longest x2 31.1 us: attn_backward(): call(body, (sds(g_shape, BF16), sds((rows, d), F32)), (ANY, WHOLE), [SMEM...]
    while x8 -> x0, blocking collectives: 92.6 us -> none
  transfers between devices with their start and end apart: 29 -> 69, of which waited for: 25 -> 37; matrix products, arithmetic and copies ran while one was open for 13% -> 14% of each run, Pallas kernels for 0% -> 29%
where the time goes in v1:
time: 419 us; the launch traced here: 413 us
  waiting for transfers between devices  136 us (32%)
  Pallas kernels  121 us (29%)
  starting transfers between devices  70.3 us (17%)
  local copies, waits for them, and re-layouts  36.5 us (9%)
  other arithmetic  34.6 us (8%)
  between operations  15.2 us (4%)
    ppermute x68, waiting for transfers between devices, swap(): return lax.ppermute(value, axis, [(i, i ^ bit) for i in range(size)])  136 us
    ppermute x68, starting transfers between devices, swap(): return lax.ppermute(value, axis, [(i, i ^ bit) for i in range(size)])  70.2 us
    pallas_call x2, Pallas kernels, attn_backward(): call(body, (sds(g_shape, BF16), sds((rows, d), F32)), (ANY, WHOLE), [SMEM...  31.1 us
    pallas_call x2, Pallas kernels, mlp_backward(): call(body, (sds(g_shape, BF16), sds((rows, d), F32)), (ANY, WHOLE), [SMEM...  23.5 us
    convert_element_type x11, other arithmetic, low_add(): return add(*parts).astype(BF16)  19 us
    pallas_call x1, Pallas kernels, mlp_forward(): call(body, outs, (ANY, ANY, ANY) + (WHOLE,) * 10, [SMEM] + [WHOLE] * 4 +...  17.8 us
    pallas_call x1, Pallas kernels, attn_forward(): call(body, outs, (ANY,) + (WHOLE,) * 10, [SMEM, WHOLE, WHOLE] + [ANY] * n...  15.4 us
    pallas_call x1, Pallas kernels, lead_backward(): call(body, (sds((rows, d), F32), sds((d, d), F32), sds((d, d), F32), sds(...  10.7 us
  transfers between devices with their start and end apart: 69, of which 37 were waited for; matrix products, arithmetic and copies ran while one was open for 14% of the time, Pallas kernels for 29%

profile of v1, /device:TPU:0, one launch (start us, length us, event | category | flops | bytes accessed | tf_op | source)
XLA Modules:
  0.0 413.2 jit_solution(6157552324379737314)
XLA Ops:
  8.0 3.0 collective-permute-start
  16.1 2.7 collective-permute-start.7
  18.7 1.6 collective-permute-start.6
  20.6 1.6 collective-permute-start.5
  22.7 3.6 collective-permute-start.3
  28.3 5.4 %collective-permute-done.3 = bf16[1,96,768]{2,1,0:T(8,128)(2,1)S(1)} collective-permute-done((bf16[1,96,768]{2,1,0:T(8,128)(2,1)S(1)}, bf16[1,96,768]{2,1,0:T(8,128)(2,1)S(1)}, u32[]{:S(2)}, u32[]{:S(2)}) %collective-permute-start.3) | collective-permute-done | bytes 147488 | tf_op jit(solution)/shard_map/ppermute | solution.py:768
  33.8 16.1 %collective-permute-done.2 = bf16[1,96,768]{2,1,0:T(8,128)(2,1)S(1)} collective-permute-done((bf16[1,96,768]{2,1,0:T(8,128)(2,1)S(1)}, bf16[1,96,768]{2,1,0:T(8,128)(2,1)S(1)}, u32[]{:S(2)}, u32[]{:S(2)}) %collective-permute-start.2) | collective-permute-done | bytes 147488 | tf_op jit(solution)/shard_map/ppermute | solution.py:768
  51.1 1.5 collective-permute-start.14
  54.1 9.2 %collective-permute-start.11 = (bf16[2,96,768]{2,1,0:T(8,128)(2,1)S(1)}, bf16[2,96,768]{2,1,0:T(8,128)(2,1)S(1)}, u32[]{:S(2)}, u32[]{:S(2)}) collective-permute-start(bf16[2,96,768]{2,1,0:T(8,128)(2,1)S(1)} %pad_maximum_fusion.10.refs_0_), channel_id=1, source_target_pairs={{0,24},{4,28},{8,16},{12,20},{16,8},{20,12},{24,0},{28,4},{1,25},{... | collective-permute-start | bytes 884744 | tf_op jit(solution)/shard_map/ppermute | solution.py:768
  63.3 3.1 collective-permute-start.9
  66.4 7.2 %collective-permute-done.11 = bf16[2,96,768]{2,1,0:T(8,128)(2,1)S(1)} collective-permute-done((bf16[2,96,768]{2,1,0:T(8,128)(2,1)S(1)}, bf16[2,96,768]{2,1,0:T(8,128)(2,1)S(1)}, u32[]{:S(2)}, u32[]{:S(2)}) %collective-permute-start.11) | collective-permute-done | bytes 294944 | tf_op jit(solution)/shard_map/ppermute | solution.py:768
  73.6 17.2 %collective-permute-done.10 = bf16[2,96,768]{2,1,0:T(8,128)(2,1)S(1)} collective-permute-done((bf16[2,96,768]{2,1,0:T(8,128)(2,1)S(1)}, bf16[2,96,768]{2,1,0:T(8,128)(2,1)S(1)}, u32[]{:S(2)}, u32[]{:S(2)}) %collective-permute-start.10) | collective-permute-done | bytes 294944 | tf_op jit(solution)/shard_map/ppermute | solution.py:768
  90.8 1.7 collective-permute-done.9
  93.2 1.9 collective-permute-start.18
  102.7 9.5 %collective-permute-done.17.refs_7_ = bf16[2,1,96,768]{3,2,1,0:T(8,128)(2,1)} collective-permute-done((bf16[2,1,96,768]{3,2,1,0:T(8,128)(2,1)S(1)}, bf16[2,1,96,768]{3,2,1,0:T(8,128)(2,1)}, u32[]{:S(2)}, u32[]{:S(2)}) %collective-permute-start.17) | collective-permute-done | bytes 294944 | tf_op jit(solution)/shard_map/ppermute | solution.py:768
  117.2 15.4 %shard_map.169 = (bf16[4,768,768]{2,1,0:T(8,128)(2,1)}, bf16[512,768]{1,0:T(8,128)(2,1)}, bf16[512,768]{1,0:T(8,128)(2,1)}, bf16[512,768]{1,0:T(8,128)(2,1)}, bf...) custom-call(s32[8]{0:T(128)} %stack.196.blk_ref, ...), custom_call_target="tpu_custom_call" | custom-call | flops 2415919104 | bytes 20000000 | tf_op jit(solution)/shard_map/pallas_call | solution.py:193
  135.0 1.6 collective-permute-start.29
  139.2 2.0 collective-permute-start.30
  141.2 2.2 collective-permute-done.30
  143.4 1.9 collective-permute-start.34
  145.5 3.0 collective-permute-start.31
  148.5 1.9 collective-permute-start.33
  150.4 4.8 %collective-permute-done.32 = bf16[2,2,8,1664]{3,2,1,0:T(8,128)(2,1)S(1)} collective-permute-done((bf16[2,2,8,1664]{3,2,1,0:T(8,128)(2,1)S(1)}, bf16[2,2,8,1664]{3,2,1,0:T(8,128)(2,1)S(1)}, u32[]{:S(2)}, u32[]{:S(2)}) %collective-permute-start.32) | collective-permute-done | bytes 106528 | tf_op jit(solution)/shard_map/ppermute | solution.py:768
  159.9 1.7 collective-permute-done.41.refs_13_
  163.5 17.8 %shard_map.170 = (bf16[2,4,768,768]{3,2,1,0:T(8,128)(2,1)}, bf16[4,640,768]{2,1,0:T(8,128)(2,1)}, bf16[4,640,768]{2,1,0:T(8,128)(2,1)}, bf16[768,512]{1,0:T(8,12...) custom-call(s32[8]{0:T(128)} %stack.196.blk_ref, ...), custom_call_target="tpu_custom_call" | custom-call | flops 6039797760 | bytes 40000000 | tf_op jit(solution)/shard_map/pallas_call | solution.py:303
  181.4 11.6 %shard_map.174 = (bf16[2,8,2,96,768]{4,3,2,1,0:T(8,128)(2,1)}, f32[512,768]{1,0:T(8,128)}) custom-call(s32[8]{0:T(128)} %stack.196.blk_ref, bf16[512,768]{1,0:T(8,128)(2,1)} %get-tuple-element.133.dm_ref, bf16[768,512]{1,0:T(8,128)(2,1)} %get-tuple-element.134.dmt_ref, bf16[768,512]{1,0:T(8,128)(2,1)} %get-tuple-element.135.ybt_ref, ...), custom_call_target="tpu_custom_call" | custom-call | flops 4831838208 | bytes 20000000 | tf_op jit(solution)/shard_map/pallas_call | solution.py:382
  193.8 2.2 copy.115
  197.2 3.4 shard_map.171
  204.5 1.6 slice.414
  206.1 4.4 %collective-permute-done.45.a1_ref = bf16[128,768]{1,0:T(8,128)(2,1)S(1)} collective-permute-done((bf16[128,768]{1,0:T(8,128)(2,1)S(1)}, bf16[128,768]{1,0:T(8,128)(2,1)S(1)}, u32[]{:S(2)}, u32[]{:S(2)}) %collective-permute-start.45) | collective-permute-done | bytes 196640 | tf_op jit(solution)/shard_map/ppermute | solution.py:768
  211.2 3.6 shard_map.172
  214.8 1.6 collective-permute-done.46
  218.7 5.8 %collective-permute-done.47.m1_ref = bf16[128,768]{1,0:T(8,128)(2,1)S(1)} collective-permute-done((bf16[128,768]{1,0:T(8,128)(2,1)S(1)}, bf16[128,768]{1,0:T(8,128)(2,1)S(1)}, u32[]{:S(2)}, u32[]{:S(2)}) %collective-permute-start.47) | collective-permute-done | bytes 196640 | tf_op jit(solution)/shard_map/ppermute | solution.py:768
  225.1 5.7 %shard_map.173 = (bf16[128,768]{1,0:T(8,128)(2,1)}, f32[128,768]{1,0:T(8,128)}, f32[768,768]{1,0:T(8,128)}, f32[768,768]{1,0:T(8,128)}, bf16[128,768]{1,0:T(8,128)(2,1)}, /*index=5*/f32[8,768]{1,0:T(8,128)}) custom-call(f32[128,768]{1,0:T(8,128)} %get-tuple-element.128.y_ref, bf16[128,768]{1,0:T(8,128)(2,1)} %copy-done.7, bf16[128,768]{1,0:T(8,128)(2,1)} %copy-done.17, ...), custom_call_target="tpu_custom_call" | custom-call | flops 603979776 | bytes 9000000 | tf_op jit(solution)/shard_map/pallas_call | solution.py:636
  230.8 1.6 collective-permute-done.48
  234.7 5.8 %collective-permute-done.49.d1_ref = bf16[128,768]{1,0:T(8,128)(2,1)S(1)} collective-permute-done((bf16[128,768]{1,0:T(8,128)(2,1)S(1)}, bf16[128,768]{1,0:T(8,128)(2,1)S(1)}, u32[]{:S(2)}, u32[]{:S(2)}) %collective-permute-start.49) | collective-permute-done | bytes 196640 | tf_op jit(solution)/shard_map/ppermute | solution.py:768
  241.2 5.3 %shard_map.176 = (f32[128,768]{1,0:T(8,128)}, bf16[128,768]{1,0:T(8,128)(2,1)}, f32[768,768]{1,0:T(8,128)}, f32[8,768]{1,0:T(8,128)}) custom-call(f32[128,768]{1,0:T(8,128)} %get-tuple-element.142.dh2_ref, bf16[128,768]{1,0:T(8,128)(2,1)} %copy-done.5, bf16[128,768]{1,0:T(8,128)(2,1)} %copy-done.14, f32[128,768]{1,0:T(8,128)} %get-tuple-element.144.n_ref, ...), custom_call_target="tpu_custom_call" | custom-call | flops 301989888 | bytes 6000000 | tf_op jit(solution)/shard_map/pallas_call | solution.py:700
  246.5 1.6 collective-permute-done.50
  250.4 11.9 %shard_map.175 = (bf16[2,8,2,96,768]{4,3,2,1,0:T(8,128)(2,1)}, f32[512,768]{1,0:T(8,128)}) custom-call(s32[8]{0:T(128)} %stack.196.blk_ref, bf16[512,768]{1,0:T(8,128)(2,1)} %get-tuple-element.133.dm_ref, bf16[768,512]{1,0:T(8,128)(2,1)} %get-tuple-element.134.dmt_ref, bf16[768,512]{1,0:T(8,128)(2,1)} %get-tuple-element.135.ybt_ref, ...), custom_call_target="tpu_custom_call" | custom-call | flops 4831838208 | bytes 20000000 | tf_op jit(solution)/shard_map/pallas_call | solution.py:382
  263.0 10.7 %shard_map.177 = (f32[128,768]{1,0:T(8,128)}, f32[768,768]{1,0:T(8,128)}, f32[768,768]{1,0:T(8,128)}, f32[16,768]{1,0:T(8,128)}) custom-call(f32[128,768]{1,0:T(8,128)} %get-tuple-element.149.dh_ref, bf16[128,768]{1,0:T(8,128)(2,1)} %copy-done.4, bf16[128,768]{1,0:T(8,128)(2,1)} %copy-done.13, bf16[128,128]{1,0:T(8,128)(2,1)} %slice.412.oh_ref, ...), custom_call_target="tpu_custom_call" | custom-call | flops 1509949440 | bytes 14000000 | tf_op jit(solution)/shard_map/pallas_call | solution.py:750
  275.1 4.4 %shard_map.178 = (f32[512,768]{1,0:T(8,128)}, bf16[512,768]{1,0:T(8,128)(2,1)}, bf16[768,512]{1,0:T(8,128)(2,1)}, f32[8,768]{1,0:T(8,128)}) custom-call(f32[512,768]{1,0:T(8,128)} %get-tuple-element.141.dy_ref, f32[4,8,768]{2,1,0:T(8,128)} %broadcast_in_dim.21.ld_ref, bf16[512,768]{1,0:T(8,128)(2,1)} %get-tuple-element.155.n_ref, ...), custom_call_target="tpu_custom_call" | custom-call | flops 7864320 | bytes 8000000 | tf_op jit(solution)/shard_map/pallas_call | solution.py:424
  279.6 15.7 %shard_map.179 = (bf16[2,8,1,112,768]{4,3,2,1,0:T(8,128)(2,1)}, f32[512,768]{1,0:T(8,128)}) custom-call(s32[8]{0:T(128)} %stack.196.blk_ref, bf16[512,768]{1,0:T(8,128)(2,1)} %get-tuple-element.158.da_ref, bf16[768,512]{1,0:T(8,128)(2,1)} %get-tuple-element.159.dat_ref, bf16[768,512]{1,0:T(8,128)(2,1)} %get-tuple-element.160.xt_ref, ...), custom_call_target="tpu_custom_call" | custom-call | flops 2415919104 | bytes 20000000 | tf_op jit(solution)/shard_map/pallas_call | solution.py:506
  295.4 3.9 fusion.4
  301.2 1.5 scatter.4
  303.5 1.9 dynamic-slice_bitcast_fusion
  305.4 10.0 %collective-permute-done.63 = bf16[2,2,96,768]{3,2,1,0:T(8,128)(2,1)} collective-permute-done((bf16[2,2,96,768]{3,2,1,0:T(8,128)(2,1)}, bf16[2,2,96,768]{3,2,1,0:T(8,128)(2,1)}, u32[]{:S(2)}, u32[]{:S(2)}) %collective-permute-start.63) | collective-permute-done | bytes 589856 | tf_op jit(solution)/shard_map/ppermute | solution.py:768
  315.6 2.4 fusion.1
  320.9 1.7 collective-permute-start.62
  323.4 15.4 %shard_map.180 = (bf16[2,8,1,112,768]{4,3,2,1,0:T(8,128)(2,1)}, f32[512,768]{1,0:T(8,128)}) custom-call(s32[8]{0:T(128)} %stack.196.blk_ref, bf16[512,768]{1,0:T(8,128)(2,1)} %get-tuple-element.158.da_ref, bf16[768,512]{1,0:T(8,128)(2,1)} %get-tuple-element.159.dat_ref, bf16[768,512]{1,0:T(8,128)(2,1)} %get-tuple-element.160.xt_ref, ...), custom_call_target="tpu_custom_call" | custom-call | flops 2415919104 | bytes 20000000 | tf_op jit(solution)/shard_map/pallas_call | solution.py:506
  341.7 1.4 collective-permute-start.53
  344.1 4.3 %collective-permute-done.64 = bf16[4,2,96,768]{3,2,1,0:T(8,128)(2,1)} collective-permute-done((bf16[4,2,96,768]{3,2,1,0:T(8,128)(2,1)}, bf16[4,2,96,768]{3,2,1,0:T(8,128)(2,1)}, u32[]{:S(2)}, u32[]{:S(2)}) %collective-permute-start.64) | collective-permute-done | bytes 1179680 | tf_op jit(solution)/shard_map/ppermute | solution.py:768
  348.4 1.7 collective-permute-done.62
  350.1 3.2 fusion.10
  353.3 2.0 collective-permute-start.65
  355.3 1.5 collective-permute-start.66
  361.4 1.5 collective-permute-start.54
  365.5 3.2 collective-permute-done.67
  368.6 10.9 %collective-permute-done.66 = bf16[2,96,768]{2,1,0:T(8,128)(2,1)} collective-permute-done((bf16[2,96,768]{2,1,0:T(8,128)(2,1)}, bf16[2,96,768]{2,1,0:T(8,128)(2,1)}, u32[]{:S(2)}, u32[]{:S(2)}) %collective-permute-start.66) | collective-permute-done | bytes 294944 | tf_op jit(solution)/shard_map/ppermute | solution.py:768
  379.5 1.7 fusion.13
  382.5 1.8 fusion.20
  384.3 1.4 collective-permute-start.59
  385.7 2.0 collective-permute-start.58
  390.6 3.1 collective-permute-done.59
  393.7 6.7 %collective-permute-done.58 = bf16[1,112,768]{2,1,0:T(8,128)(2,1)S(1)} collective-permute-done((bf16[1,112,768]{2,1,0:T(8,128)(2,1)S(1)}, bf16[1,112,768]{2,1,0:T(8,128)(2,1)S(1)}, u32[]{:S(2)}, u32[]{:S(2)}) %collective-permute-start.58) | collective-permute-done | bytes 172064 | tf_op jit(solution)/shard_map/ppermute | solution.py:768
  (259 shorter events, 79.9 us)
Async XLA Ops:
  7.2 186.6 %all-gather.3.cloned.1.call-start = ((), (), s32[]{:S(2)}) async-start(), calls=%async_computation | async-start | bytes 3981312 | tf_op jit(solution)/shard_map/all_gather | solution.py:862
  8.0 8.1 %collective-permute-start = (bf16[16,96]{1,0:T(8,128)(2,1)S(1)}, bf16[16,96]{1,0:T(8,128)(2,1)S(1)}, u32[]{:S(2)}, u32[]{:S(2)}) collective-permute-start(bf16[16,96]{1,0:T(8,128)(2,1)S(1)} %get-tuple-element.253), channel_id=1, source_target_pairs={{0,4},{4,0},{8,12},{12,8},{16,20},{20,16},{24,28},{28,24},{1,5},{5... | collective-permute-start | bytes 9224 | tf_op jit(solution)/shard_map/ppermute | solution.py:768
  16.1 6.7 %collective-permute-start.7 = (bf16[2,16,96]{2,1,0:T(8,128)(2,1)S(1)}, bf16[2,16,96]{2,1,0:T(8,128)(2,1)S(1)}, u32[]{:S(2)}, u32[]{:S(2)}) collective-permute-start(bf16[2,16,96]{2,1,0:T(8,128)(2,1)S(1)} %get-tuple-element.247), channel_id=1, source_target_pairs={{0,16},{4,20},{8,24},{12,28},{16,0},{20,4},{24,8},{28,12},{1,17},{... | collective-permute-start | bytes 18440 | tf_op jit(solution)/shard_map/ppermute | solution.py:768
  18.7 7.6 %collective-permute-start.6 = (bf16[2,16,96]{2,1,0:T(8,128)(2,1)S(1)}, bf16[2,16,96]{2,1,0:T(8,128)(2,1)S(1)}, u32[]{:S(2)}, u32[]{:S(2)}) collective-permute-start(bf16[2,16,96]{2,1,0:T(8,128)(2,1)S(1)} %get-tuple-element.247), channel_id=1, source_target_pairs={{0,8},{4,12},{8,0},{12,4},{16,24},{20,28},{24,16},{28,20},{1,9},{5... | collective-permute-start | bytes 18440 | tf_op jit(solution)/shard_map/ppermute | solution.py:768
  20.3 6.1 %collective-permute-start.8 = (bf16[2,16,96]{2,1,0:T(8,128)(2,1)S(1)}, bf16[2,16,96]{2,1,0:T(8,128)(2,1)S(1)}, u32[]{:S(2)}, u32[]{:S(2)}) collective-permute-start(bf16[2,16,96]{2,1,0:T(8,128)(2,1)S(1)} %get-tuple-element.247), channel_id=1, source_target_pairs={{0,24},{4,28},{8,16},{12,20},{16,8},{20,12},{24,0},{28,4},{1,25},{... | collective-permute-start | bytes 18440 | tf_op jit(solution)/shard_map/ppermute | solution.py:768
  20.6 6.6 %collective-permute-start.5 = (bf16[1,96,768]{2,1,0:T(8,128)(2,1)S(1)}, bf16[1,96,768]{2,1,0:T(8,128)(2,1)S(1)}, u32[]{:S(2)}, u32[]{:S(2)}) collective-permute-start(bf16[1,96,768]{2,1,0:T(8,128)(2,1)S(1)} %maximum_bitcast_fusion.3.refs_0_), channel_id=1, source_target_pairs={{0,2},{1,3},{2,0},{3,1},{4,6},{5,7},{6,4},{7,5},{8,10},{9,11},{10,... | collective-permute-start | bytes 442376 | tf_op jit(solution)/shard_map/ppermute | solution.py:768
  22.2 6.1 %collective-permute-start.4 = (bf16[1,96,768]{2,1,0:T(8,128)(2,1)S(1)}, bf16[1,96,768]{2,1,0:T(8,128)(2,1)S(1)}, u32[]{:S(2)}, u32[]{:S(2)}) collective-permute-start(bf16[1,96,768]{2,1,0:T(8,128)(2,1)S(1)} %maximum_bitcast_fusion.3.refs_0_), channel_id=1, source_target_pairs={{0,4},{4,0},{8,12},{12,8},{16,20},{20,16},{24,28},{28,24},{1,5},{5... | collective-permute-start | bytes 442376 | tf_op jit(solution)/shard_map/ppermute | solution.py:768
  22.7 11.0 %collective-permute-start.3 = (bf16[1,96,768]{2,1,0:T(8,128)(2,1)S(1)}, bf16[1,96,768]{2,1,0:T(8,128)(2,1)S(1)}, u32[]{:S(2)}, u32[]{:S(2)}) collective-permute-start(bf16[1,96,768]{2,1,0:T(8,128)(2,1)S(1)} %maximum_bitcast_fusion.3.refs_0_), channel_id=1, source_target_pairs={{0,24},{4,28},{8,16},{12,20},{16,8},{20,12},{24,0},{28,4},{1,25},{... | collective-permute-start | bytes 442376 | tf_op jit(solution)/shard_map/ppermute | solution.py:768
  26.4 23.5 %collective-permute-start.2 = (bf16[1,96,768]{2,1,0:T(8,128)(2,1)S(1)}, bf16[1,96,768]{2,1,0:T(8,128)(2,1)S(1)}, u32[]{:S(2)}, u32[]{:S(2)}) collective-permute-start(bf16[1,96,768]{2,1,0:T(8,128)(2,1)S(1)} %maximum_bitcast_fusion.3.refs_0_), channel_id=1, source_target_pairs={{0,16},{4,20},{8,24},{12,28},{16,0},{20,4},{24,8},{28,12},{1,17},{... | collective-permute-start | bytes 442376 | tf_op jit(solution)/shard_map/ppermute | solution.py:768
  26.4 23.5 %collective-permute-start.1 = (bf16[1,96,768]{2,1,0:T(8,128)(2,1)S(1)}, bf16[1,96,768]{2,1,0:T(8,128)(2,1)S(1)}, u32[]{:S(2)}, u32[]{:S(2)}) collective-permute-start(bf16[1,96,768]{2,1,0:T(8,128)(2,1)S(1)} %maximum_bitcast_fusion.3.refs_0_), channel_id=1, source_target_pairs={{0,8},{4,12},{8,0},{12,4},{16,24},{20,28},{24,16},{28,20},{1,9},{5... | collective-permute-start | bytes 442376 | tf_op jit(solution)/shard_map/ppermute | solution.py:768
  49.9 13.4 %collective-permute-start.15 = (bf16[2,96,768]{2,1,0:T(8,128)(2,1)S(1)}, bf16[2,96,768]{2,1,0:T(8,128)(2,1)S(1)}, u32[]{:S(2)}, u32[]{:S(2)}) collective-permute-start(bf16[2,96,768]{2,1,0:T(8,128)(2,1)S(1)} %pad_maximum_fusion.10.refs_0_), channel_id=1, source_target_pairs={{0,2},{1,3},{2,0},{3,1},{4,6},{5,7},{6,4},{7,5},{8,10},{9,11},{10,... | collective-permute-start | bytes 884744 | tf_op jit(solution)/shard_map/ppermute | solution.py:768
  51.1 12.2 %collective-permute-start.14 = (bf16[2,96,768]{2,1,0:T(8,128)(2,1)S(1)}, bf16[2,96,768]{2,1,0:T(8,128)(2,1)}, u32[]{:S(2)}, u32[]{:S(2)}) collective-permute-start(bf16[2,96,768]{2,1,0:T(8,128)(2,1)S(1)} %pad_maximum_fusion.10.refs_0_), channel_id=1, source_target_pairs={{0,4},{4,0},{8,12},{12,8},{16,20},{20,16},{24,28},{28,24},{1,5},{5... | collective-permute-start | bytes 884744 | tf_op jit(solution)/shard_map/ppermute | solution.py:768
  52.6 39.9 %collective-permute-start.13 = (bf16[3,1,96,768]{3,2,1,0:T(8,128)(2,1)S(1)}, bf16[3,1,96,768]{3,2,1,0:T(8,128)(2,1)}, u32[]{:S(2)}, u32[]{:S(2)}) collective-permute-start(bf16[3,1,96,768]{3,2,1,0:T(8,128)(2,1)S(1)} %pad_maximum_fusion.8.refs_1_), channel_id=1, source_target_pairs={{0,2},{1,3},{2,0},{3,1},{4,6},{5,7},{6,4},{7,5},{8,10},{9,11},{10,... | collective-permute-start | bytes 1327112 | tf_op jit(solution)/shard_map/ppermute | solution.py:768
  53.8 38.8 %collective-permute-start.12 = (bf16[3,1,96,768]{3,2,1,0:T(8,128)(2,1)S(1)}, bf16[3,1,96,768]{3,2,1,0:T(8,128)(2,1)S(1)}, u32[]{:S(2)}, u32[]{:S(2)}) collective-permute-start(bf16[3,1,96,768]{3,2,1,0:T(8,128)(2,1)S(1)} %pad_maximum_fusion.8.refs_1_), channel_id=1, source_target_pairs={{0,4},{4,0},{8,12},{12,8},{16,20},{20,16},{24,28},{28,24},{1,5},{5... | collective-permute-start | bytes 1327112 | tf_op jit(solution)/shard_map/ppermute | solution.py:768
  54.1 19.5 %collective-permute-start.11 = (bf16[2,96,768]{2,1,0:T(8,128)(2,1)S(1)}, bf16[2,96,768]{2,1,0:T(8,128)(2,1)S(1)}, u32[]{:S(2)}, u32[]{:S(2)}) collective-permute-start(bf16[2,96,768]{2,1,0:T(8,128)(2,1)S(1)} %pad_maximum_fusion.10.refs_0_), channel_id=1, source_target_pairs={{0,24},{4,28},{8,16},{12,20},{16,8},{20,12},{24,0},{28,4},{1,25},{... | collective-permute-start | bytes 884744 | tf_op jit(solution)/shard_map/ppermute | solution.py:768
  63.3 27.5 %collective-permute-start.10 = (bf16[2,96,768]{2,1,0:T(8,128)(2,1)S(1)}, bf16[2,96,768]{2,1,0:T(8,128)(2,1)S(1)}, u32[]{:S(2)}, u32[]{:S(2)}) collective-permute-start(bf16[2,96,768]{2,1,0:T(8,128)(2,1)S(1)} %pad_maximum_fusion.10.refs_0_), channel_id=1, source_target_pairs={{0,16},{4,20},{8,24},{12,28},{16,0},{20,4},{24,8},{28,12},{1,17},{... | collective-permute-start | bytes 884744 | tf_op jit(solution)/shard_map/ppermute | solution.py:768
  63.3 29.2 %collective-permute-start.9 = (bf16[2,96,768]{2,1,0:T(8,128)(2,1)S(1)}, bf16[2,96,768]{2,1,0:T(8,128)(2,1)S(1)}, u32[]{:S(2)}, u32[]{:S(2)}) collective-permute-start(bf16[2,96,768]{2,1,0:T(8,128)(2,1)S(1)} %pad_maximum_fusion.10.refs_0_), channel_id=1, source_target_pairs={{0,8},{4,12},{8,0},{12,4},{16,24},{20,28},{24,16},{28,20},{1,9},{5... | collective-permute-start | bytes 884744 | tf_op jit(solution)/shard_map/ppermute | solution.py:768
  92.7 20.1 %collective-permute-start.19 = (bf16[3,2,96,768]{3,2,1,0:T(8,128)(2,1)S(1)}, bf16[3,2,96,768]{3,2,1,0:T(8,128)(2,1)}, u32[]{:S(2)}, u32[]{:S(2)}) collective-permute-start(bf16[3,2,96,768]{3,2,1,0:T(8,128)(2,1)S(1)} %pad_maximum_fusion.2.refs_1_), channel_id=1, source_target_pairs={{0,2},{1,3},{2,0},{3,1},{4,6},{5,7},{6,4},{7,5},{8,10},{9,11},{10,... | collective-permute-start | bytes 2654216 | tf_op jit(solution)/shard_map/ppermute | solution.py:768
  93.2 20.1 %collective-permute-start.18 = (bf16[3,2,96,768]{3,2,1,0:T(8,128)(2,1)S(1)}, bf16[3,2,96,768]{3,2,1,0:T(8,128)(2,1)S(1)}, u32[]{:S(2)}, u32[]{:S(2)}) collective-permute-start(bf16[3,2,96,768]{3,2,1,0:T(8,128)(2,1)S(1)} %pad_maximum_fusion.2.refs_1_), channel_id=1, source_target_pairs={{0,4},{4,0},{8,12},{12,8},{16,20},{20,16},{24,28},{28,24},{1,5},{5... | collective-permute-start | bytes 2654216 | tf_op jit(solution)/shard_map/ppermute | solution.py:768
  95.1 18.3 %collective-permute-start.20 = (bf16[1,96,768]{2,1,0:T(8,128)(2,1)S(1)}, bf16[1,96,768]{2,1,0:T(8,128)(2,1)}, u32[]{:S(2)}, u32[]{:S(2)}) collective-permute-start(bf16[1,96,768]{2,1,0:T(8,128)(2,1)S(1)} %maximum_bitcast_fusion.3.refs_0_), channel_id=1, source_target_pairs={{0,1},{1,0},{2,3},{3,2},{4,5},{5,4},{6,7},{7,6},{8,9},{9,8},{10,11... | collective-permute-start | bytes 442376 | tf_op jit(solution)/shard_map/ppermute | solution.py:768
  98.8 13.4 %collective-permute-start.17 = (bf16[2,1,96,768]{3,2,1,0:T(8,128)(2,1)S(1)}, bf16[2,1,96,768]{3,2,1,0:T(8,128)(2,1)}, u32[]{:S(2)}, u32[]{:S(2)}) collective-permute-start(bf16[2,1,96,768]{3,2,1,0:T(8,128)(2,1)S(1)} %slice.319), channel_id=1, source_target_pairs={{0,2},{1,3},{2,0},{3,1},{4,6},{5,7},{6,4},{7,5},{8,10},{9,11},{10,... | collective-permute-start | bytes 884744 | tf_op jit(solution)/shard_map/ppermute | solution.py:768
  100.1 12.6 %collective-permute-start.16 = (bf16[2,1,96,768]{3,2,1,0:T(8,128)(2,1)S(1)}, bf16[2,1,96,768]{3,2,1,0:T(8,128)(2,1)}, u32[]{:S(2)}, u32[]{:S(2)}) collective-permute-start(bf16[2,1,96,768]{3,2,1,0:T(8,128)(2,1)S(1)} %pad_maximum_fusion.11), channel_id=1, source_target_pairs={{0,4},{4,0},{8,12},{12,8},{16,20},{20,16},{24,28},{28,24},{1,5},{5... | collective-permute-start | bytes 884744 | tf_op jit(solution)/shard_map/ppermute | solution.py:768
  112.2 2.2 collective-permute-start.23
  112.8 3.0 collective-permute-start.21
  113.3 2.8 collective-permute-start.24
  113.4 2.9 collective-permute-start.25
  114.3 2.5 collective-permute-start.26
  114.4 2.7 collective-permute-start.27
  135.0 4.2 %collective-permute-start.29 = (bf16[2,8,1664]{2,1,0:T(8,128)(2,1)S(1)}, bf16[2,8,1664]{2,1,0:T(8,128)(2,1)S(1)}, u32[]{:S(2)}, u32[]{:S(2)}) collective-permute-start(bf16[2,8,1664]{2,1,0:T(8,128)(2,1)S(1)} %add_dynamic-update-slice_fusion), channel_id=1, source_target_pairs={{0,2},{1,3},{2,0},{3,1},{4,6},{5,7},{6,4},{7,5},{8,10},{9,11},{10,... | collective-permute-start | bytes 159752 | tf_op jit(solution)/shard_map/ppermute | solution.py:768
  136.6 8.7 %collective-permute-start.36 = (bf16[2,96,768]{2,1,0:T(8,128)(2,1)S(1)}, bf16[2,96,768]{2,1,0:T(8,128)(2,1)S(1)}, u32[]{:S(2)}, u32[]{:S(2)}) collective-permute-start(bf16[2,96,768]{2,1,0:T(8,128)(2,1)S(1)} %pad_maximum_fusion.10.refs_0_), channel_id=1, source_target_pairs={{0,1},{1,0},{2,3},{3,2},{4,5},{5,4},{6,7},{7,6},{8,9},{9,8},{10,11... | collective-permute-start | bytes 884744 | tf_op jit(solution)/shard_map/ppermute | solution.py:768
  136.7 8.8 %collective-permute-start.38 = (bf16[2,96,768]{2,1,0:T(8,128)(2,1)}, bf16[2,96,768]{2,1,0:T(8,128)(2,1)S(1)}, u32[]{:S(2)}, u32[]{:S(2)}) collective-permute-start(bf16[2,96,768]{2,1,0:T(8,128)(2,1)} %collective-permute-done.14.refs_2_), channel_id=1, source_target_pairs={{0,1},{1,0},{2,3},{3,2},{4,5},{5,4},{6,7},{7,6},{8,9},{9,8},{10,11... | collective-permute-start | bytes 884744 | tf_op jit(solution)/shard_map/ppermute | solution.py:768
  137.1 11.3 %collective-permute-start.39 = (bf16[2,96,768]{2,1,0:T(8,128)(2,1)S(1)}, bf16[2,96,768]{2,1,0:T(8,128)(2,1)S(1)}, u32[]{:S(2)}, u32[]{:S(2)}) collective-permute-start(bf16[2,96,768]{2,1,0:T(8,128)(2,1)S(1)} %collective-permute-done.15.refs_3_), channel_id=1, source_target_pairs={{0,1},{1,0},{2,3},{3,2},{4,5},{5,4},{6,7},{7,6},{8,9},{9,8},{10,11... | collective-permute-start | bytes 884744 | tf_op jit(solution)/shard_map/ppermute | solution.py:768
  138.2 18.2 %collective-permute-start.35 = (bf16[2,2,96,768]{3,2,1,0:T(8,128)(2,1)S(1)}, bf16[2,2,96,768]{3,2,1,0:T(8,128)(2,1)S(1)}, u32[]{:S(2)}, u32[]{:S(2)}) collective-permute-start(bf16[2,2,96,768]{3,2,1,0:T(8,128)(2,1)S(1)} %slice.324), channel_id=1, source_target_pairs={{0,2},{1,3},{2,0},{3,1},{4,6},{5,7},{6,4},{7,5},{8,10},{9,11},{10,... | collective-permute-start | bytes 1769480 | tf_op jit(solution)/shard_map/ppermute | solution.py:768
  139.2 4.2 %collective-permute-start.30 = (bf16[2,8,1664]{2,1,0:T(8,128)(2,1)S(1)}, bf16[2,8,1664]{2,1,0:T(8,128)(2,1)S(1)}, u32[]{:S(2)}, u32[]{:S(2)}) collective-permute-start(bf16[2,8,1664]{2,1,0:T(8,128)(2,1)S(1)} %add.416), channel_id=1, source_target_pairs={{0,4},{4,0},{8,12},{12,8},{16,20},{20,16},{24,28},{28,24},{1,5},{5... | collective-permute-start | bytes 159752 | tf_op jit(solution)/shard_map/ppermute | solution.py:768
  143.4 14.3 %collective-permute-start.34 = (bf16[2,2,96,768]{3,2,1,0:T(8,128)(2,1)S(1)}, bf16[2,2,96,768]{3,2,1,0:T(8,128)(2,1)S(1)}, u32[]{:S(2)}, u32[]{:S(2)}) collective-permute-start(bf16[2,2,96,768]{3,2,1,0:T(8,128)(2,1)S(1)} %pad_maximum_fusion.3), channel_id=1, source_target_pairs={{0,4},{4,0},{8,12},{12,8},{16,20},{20,16},{24,28},{28,24},{1,5},{5... | collective-permute-start | bytes 1769480 | tf_op jit(solution)/shard_map/ppermute | solution.py:768
  145.4 9.8 %collective-permute-start.32 = (bf16[2,2,8,1664]{3,2,1,0:T(8,128)(2,1)S(1)}, bf16[2,2,8,1664]{3,2,1,0:T(8,128)(2,1)S(1)}, u32[]{:S(2)}, u32[]{:S(2)}) collective-permute-start(bf16[2,2,8,1664]{3,2,1,0:T(8,128)(2,1)S(1)} %get-tuple-element.243), channel_id=1, source_target_pairs={{0,16},{4,20},{8,24},{12,28},{16,0},{20,4},{24,8},{28,12},{1,17},{... | collective-permute-start | bytes 319496 | tf_op jit(solution)/shard_map/ppermute | solution.py:768
  145.5 9.7 %collective-permute-start.31 = (bf16[2,2,8,1664]{3,2,1,0:T(8,128)(2,1)S(1)}, bf16[2,2,8,1664]{3,2,1,0:T(8,128)(2,1)S(1)}, u32[]{:S(2)}, u32[]{:S(2)}) collective-permute-start(bf16[2,2,8,1664]{3,2,1,0:T(8,128)(2,1)S(1)} %get-tuple-element.243), channel_id=1, source_target_pairs={{0,8},{4,12},{8,0},{12,4},{16,24},{20,28},{24,16},{28,20},{1,9},{5... | collective-permute-start | bytes 319496 | tf_op jit(solution)/shard_map/ppermute | solution.py:768
  148.5 8.0 %collective-permute-start.33 = (bf16[2,2,8,1664]{3,2,1,0:T(8,128)(2,1)S(1)}, bf16[2,2,8,1664]{3,2,1,0:T(8,128)(2,1)S(1)}, u32[]{:S(2)}, u32[]{:S(2)}) collective-permute-start(bf16[2,2,8,1664]{3,2,1,0:T(8,128)(2,1)S(1)} %get-tuple-element.243), channel_id=1, source_target_pairs={{0,24},{4,28},{8,16},{12,20},{16,8},{20,12},{24,0},{28,4},{1,25},{... | collective-permute-start | bytes 319496 | tf_op jit(solution)/shard_map/ppermute | solution.py:768
  155.1 3.5 collective-permute-start.37
  155.2 3.7 collective-permute-start.40
  156.4 5.1 %collective-permute-start.41 = (bf16[3,2,96,768]{3,2,1,0:T(8,128)(2,1)}, bf16[3,2,96,768]{3,2,1,0:T(8,128)(2,1)S(1)}, u32[]{:S(2)}, u32[]{:S(2)}) collective-permute-start(bf16[3,2,96,768]{3,2,1,0:T(8,128)(2,1)} %collective-permute-done.19.refs_5_), channel_id=1, source_target_pairs={{0,1},{1,0},{2,3},{3,2},{4,5},{5,4},{6,7},{7,6},{8,9},{9,8},{10,11... | collective-permute-start | bytes 2654216 | tf_op jit(solution)/shard_map/ppermute | solution.py:768
  156.4 6.1 %collective-permute-start.43 = (bf16[2,2,96,768]{3,2,1,0:T(8,128)(2,1)S(1)}, bf16[2,2,96,768]{3,2,1,0:T(8,128)(2,1)S(1)}, u32[]{:S(2)}, u32[]{:S(2)}) collective-permute-start(bf16[2,2,96,768]{3,2,1,0:T(8,128)(2,1)S(1)} %collective-permute-done.35.refs_7_), channel_id=1, source_target_pairs={{0,1},{1,0},{2,3},{3,2},{4,5},{5,4},{6,7},{7,6},{8,9},{9,8},{10,11... | collective-permute-start | bytes 1769480 | tf_op jit(solution)/shard_map/ppermute | solution.py:768
  157.7 4.8 %collective-permute-start.42 = (bf16[2,2,96,768]{3,2,1,0:T(8,128)(2,1)S(1)}, bf16[2,2,96,768]{3,2,1,0:T(8,128)(2,1)S(1)}, u32[]{:S(2)}, u32[]{:S(2)}) collective-permute-start(bf16[2,2,96,768]{3,2,1,0:T(8,128)(2,1)S(1)} %collective-permute-done.34.refs_6_), channel_id=1, source_target_pairs={{0,1},{1,0},{2,3},{3,2},{4,5},{5,4},{6,7},{7,6},{8,9},{9,8},{10,11... | collective-permute-start | bytes 1769480 | tf_op jit(solution)/shard_map/ppermute | solution.py:768
  193.0 102.4 %collective-permute-start.60 = (bf16[2,2,4,2,96,768]{5,4,3,2,1,0:T(8,128)(2,1)}, bf16[2,2,4,2,96,768]{5,4,3,2,1,0:T(8,128)(2,1)}, u32[]{:S(2)}, u32[]{:S(2)}) collective-permute-start(bf16[2,2,4,2,96,768]{5,4,3,2,1,0:T(8,128)(2,1)} %bitcast.316), channel_id=1, source_target_pairs={{0,1},{1,0},{2,3},{3,2},{4,5},{5,4},{6,7},{7,6},{8,9},{9,8},{10,11... | collective-permute-start | bytes 14155784 | tf_op jit(solution)/shard_map/ppermute | solution.py:768
  200.6 1.7 collective-permute-start.44
  203.2 7.2 %collective-permute-start.45 = (bf16[128,768]{1,0:T(8,128)(2,1)S(1)}, bf16[128,768]{1,0:T(8,128)(2,1)S(1)}, u32[]{:S(2)}, u32[]{:S(2)}) collective-permute-start(bf16[128,768]{1,0:T(8,128)(2,1)S(1)} %add_convert_fusion.11.a0_ref), channel_id=1, source_target_pairs={{0,2},{1,3},{2,0},{3,1},{4,6},{5,7},{6,4},{7,5},{8,10},{9,11},{10,... | collective-permute-start | bytes 589832 | tf_op jit(solution)/shard_map/ppermute | solution.py:768
  217.5 7.0 %collective-permute-start.47 = (bf16[128,768]{1,0:T(8,128)(2,1)S(1)}, bf16[128,768]{1,0:T(8,128)(2,1)S(1)}, u32[]{:S(2)}, u32[]{:S(2)}) collective-permute-start(bf16[128,768]{1,0:T(8,128)(2,1)S(1)} %add_convert_fusion.10.m0_ref), channel_id=1, source_target_pairs={{0,2},{1,3},{2,0},{3,1},{4,6},{5,7},{6,4},{7,5},{8,10},{9,11},{10,... | collective-permute-start | bytes 589832 | tf_op jit(solution)/shard_map/ppermute | solution.py:768
  233.5 7.0 %collective-permute-start.49 = (bf16[128,768]{1,0:T(8,128)(2,1)S(1)}, bf16[128,768]{1,0:T(8,128)(2,1)S(1)}, u32[]{:S(2)}, u32[]{:S(2)}) collective-permute-start(bf16[128,768]{1,0:T(8,128)(2,1)S(1)} %add_convert_fusion.9.d0_ref), channel_id=1, source_target_pairs={{0,2},{1,3},{2,0},{3,1},{4,6},{5,7},{6,4},{7,5},{8,10},{9,11},{10,... | collective-permute-start | bytes 589832 | tf_op jit(solution)/shard_map/ppermute | solution.py:768
  249.1 13.1 %collective-permute-start.51 = (bf16[128,768]{1,0:T(8,128)(2,1)S(1)}, bf16[128,768]{1,0:T(8,128)(2,1)S(1)}, u32[]{:S(2)}, u32[]{:S(2)}) collective-permute-start(bf16[128,768]{1,0:T(8,128)(2,1)S(1)} %add_convert_fusion.8.d0_ref), channel_id=1, source_target_pairs={{0,2},{1,3},{2,0},{3,1},{4,6},{5,7},{6,4},{7,5},{8,10},{9,11},{10,... | collective-permute-start | bytes 589832 | tf_op jit(solution)/shard_map/ppermute | solution.py:768
  295.3 43.5 %collective-permute-start.52 = (bf16[2,2,4,1,112,768]{5,4,3,2,1,0:T(8,128)(2,1)}, bf16[2,2,4,1,112,768]{5,4,3,2,1,0:T(8,128)(2,1)S(1)}, u32[]{:S(2)}, u32[]{:S(2)}) collective-permute-start(bf16[2,2,4,1,112,768]{5,4,3,2,1,0:T(8,128)(2,1)} %bitcast.317), channel_id=1, source_target_pairs={{0,1},{1,0},{2,3},{3,2},{4,5},{5,4},{6,7},{7,6},{8,9},{9,8},{10,11... | collective-permute-start | bytes 8257544 | tf_op jit(solution)/shard_map/ppermute | solution.py:768
  299.3 16.0 %collective-permute-start.63 = (bf16[2,2,96,768]{3,2,1,0:T(8,128)(2,1)}, bf16[2,2,96,768]{3,2,1,0:T(8,128)(2,1)}, u32[]{:S(2)}, u32[]{:S(2)}) collective-permute-start(bf16[2,2,96,768]{3,2,1,0:T(8,128)(2,1)} %get-tuple-element.215), channel_id=1, source_target_pairs={{0,4},{4,0},{8,12},{12,8},{16,20},{20,16},{24,28},{28,24},{1,5},{5... | collective-permute-start | bytes 1769480 | tf_op jit(solution)/shard_map/ppermute | solution.py:768
  299.8 15.8 %collective-permute-start.61 = (bf16[2,2,96,768]{3,2,1,0:T(8,128)(2,1)}, bf16[2,2,96,768]{3,2,1,0:T(8,128)(2,1)}, u32[]{:S(2)}, u32[]{:S(2)}) collective-permute-start(bf16[2,2,96,768]{3,2,1,0:T(8,128)(2,1)} %get-tuple-element.216), channel_id=1, source_target_pairs={{0,2},{1,3},{2,0},{3,1},{4,6},{5,7},{6,4},{7,5},{8,10},{9,11},{10,... | collective-permute-start | bytes 1769480 | tf_op jit(solution)/shard_map/ppermute | solution.py:768
  319.1 29.2 %collective-permute-start.64 = (bf16[4,2,96,768]{3,2,1,0:T(8,128)(2,1)}, bf16[4,2,96,768]{3,2,1,0:T(8,128)(2,1)}, u32[]{:S(2)}, u32[]{:S(2)}) collective-permute-start(bf16[4,2,96,768]{3,2,1,0:T(8,128)(2,1)} %pad_maximum_fusion.1), channel_id=1, source_target_pairs={{0,2},{1,3},{2,0},{3,1},{4,6},{5,7},{6,4},{7,5},{8,10},{9,11},{10,... | collective-permute-start | bytes 3538952 | tf_op jit(solution)/shard_map/ppermute | solution.py:768
  320.9 29.2 %collective-permute-start.62 = (bf16[4,2,96,768]{3,2,1,0:T(8,128)(2,1)}, bf16[4,2,96,768]{3,2,1,0:T(8,128)(2,1)}, u32[]{:S(2)}, u32[]{:S(2)}) collective-permute-start(bf16[4,2,96,768]{3,2,1,0:T(8,128)(2,1)} %pad_maximum_fusion), channel_id=1, source_target_pairs={{0,4},{4,0},{8,12},{12,8},{16,20},{20,16},{24,28},{28,24},{1,5},{5... | collective-permute-start | bytes 3538952 | tf_op jit(solution)/shard_map/ppermute | solution.py:768
  340.1 16.7 %collective-permute-start.55 = (bf16[2,1,112,768]{3,2,0,1:T(8,128)(2,1)S(1)}, bf16[2,1,112,768]{3,2,0,1:T(8,128)(2,1)S(1)}, u32[]{:S(2)}, u32[]{:S(2)}) collective-permute-start(bf16[2,1,112,768]{3,2,0,1:T(8,128)(2,1)S(1)} %get-tuple-element.223), channel_id=1, source_target_pairs={{0,4},{4,0},{8,12},{12,8},{16,20},{20,16},{24,28},{28,24},{1,5},{5... | collective-permute-start | bytes 1032200 | tf_op jit(solution)/shard_map/ppermute | solution.py:768
  341.7 15.1 %collective-permute-start.53 = (bf16[2,1,112,768]{3,2,0,1:T(8,128)(2,1)S(1)}, bf16[2,1,112,768]{3,2,0,1:T(8,128)(2,1)S(1)}, u32[]{:S(2)}, u32[]{:S(2)}) collective-permute-start(bf16[2,1,112,768]{3,2,0,1:T(8,128)(2,1)S(1)} %get-tuple-element.226), channel_id=1, source_target_pairs={{0,2},{1,3},{2,0},{3,1},{4,6},{5,7},{6,4},{7,5},{8,10},{9,11},{10,... | collective-permute-start | bytes 1032200 | tf_op jit(solution)/shard_map/ppermute | solution.py:768
  353.3 12.2 %collective-permute-start.65 = (bf16[2,96,768]{2,1,0:T(8,128)(2,1)}, bf16[2,96,768]{2,1,0:T(8,128)(2,1)}, u32[]{:S(2)}, u32[]{:S(2)}) collective-permute-start(bf16[2,96,768]{2,1,0:T(8,128)(2,1)} %get-tuple-element.210), channel_id=1, source_target_pairs={{0,8},{4,12},{8,0},{12,4},{16,24},{20,28},{24,16},{28,20},{1,9},{5... | collective-permute-start | bytes 884744 | tf_op jit(solution)/shard_map/ppermute | solution.py:768
  355.3 13.4 %collective-permute-start.67 = (bf16[2,96,768]{2,1,0:T(8,128)(2,1)}, bf16[2,96,768]{2,1,0:T(8,128)(2,1)}, u32[]{:S(2)}, u32[]{:S(2)}) collective-permute-start(bf16[2,96,768]{2,1,0:T(8,128)(2,1)} %get-tuple-element.211), channel_id=1, source_target_pairs={{0,24},{4,28},{8,16},{12,20},{16,8},{20,12},{24,0},{28,4},{1,25},{... | collective-permute-start | bytes 884744 | tf_op jit(solution)/shard_map/ppermute | solution.py:768
  355.3 24.2 %collective-permute-start.66 = (bf16[2,96,768]{2,1,0:T(8,128)(2,1)}, bf16[2,96,768]{2,1,0:T(8,128)(2,1)}, u32[]{:S(2)}, u32[]{:S(2)}) collective-permute-start(bf16[2,96,768]{2,1,0:T(8,128)(2,1)} %get-tuple-element.212), channel_id=1, source_target_pairs={{0,16},{4,20},{8,24},{12,28},{16,0},{20,4},{24,8},{28,12},{1,17},{... | collective-permute-start | bytes 884744 | tf_op jit(solution)/shard_map/ppermute | solution.py:768
  359.1 23.4 %collective-permute-start.56 = (bf16[4,1,112,768]{3,2,1,0:T(8,128)(2,1)}, bf16[4,1,112,768]{3,2,1,0:T(8,128)(2,1)}, u32[]{:S(2)}, u32[]{:S(2)}) collective-permute-start(bf16[4,1,112,768]{3,2,1,0:T(8,128)(2,1)} %maximum_bitcast_fusion.1), channel_id=1, source_target_pairs={{0,2},{1,3},{2,0},{3,1},{4,6},{5,7},{6,4},{7,5},{8,10},{9,11},{10,... | collective-permute-start | bytes 2064392 | tf_op jit(solution)/shard_map/ppermute | solution.py:768
  361.4 21.1 %collective-permute-start.54 = (bf16[4,1,112,768]{3,2,1,0:T(8,128)(2,1)}, bf16[4,1,112,768]{3,2,1,0:T(8,128)(2,1)}, u32[]{:S(2)}, u32[]{:S(2)}) collective-permute-start(bf16[4,1,112,768]{3,2,1,0:T(8,128)(2,1)} %maximum_bitcast_fusion), channel_id=1, source_target_pairs={{0,4},{4,0},{8,12},{12,8},{16,20},{20,16},{24,28},{28,24},{1,5},{5... | collective-permute-start | bytes 2064392 | tf_op jit(solution)/shard_map/ppermute | solution.py:768
  384.2 6.4 %collective-permute-start.57 = (bf16[1,112,768]{2,1,0:T(8,128)(2,1)S(1)}, bf16[1,112,768]{2,1,0:T(8,128)(2,1)S(1)}, u32[]{:S(2)}, u32[]{:S(2)}) collective-permute-start(bf16[1,112,768]{2,1,0:T(8,128)(2,1)S(1)} %get-tuple-element.219), channel_id=1, source_target_pairs={{0,8},{4,12},{8,0},{12,4},{16,24},{20,28},{24,16},{28,20},{1,9},{5... | collective-permute-start | bytes 516104 | tf_op jit(solution)/shard_map/ppermute | solution.py:768
  384.3 9.4 %collective-permute-start.59 = (bf16[1,112,768]{2,1,0:T(8,128)(2,1)S(1)}, bf16[1,112,768]{2,1,0:T(8,128)(2,1)S(1)}, u32[]{:S(2)}, u32[]{:S(2)}) collective-permute-start(bf16[1,112,768]{2,1,0:T(8,128)(2,1)S(1)} %get-tuple-element.220), channel_id=1, source_target_pairs={{0,24},{4,28},{8,16},{12,20},{16,8},{20,12},{24,0},{28,4},{1,25},{... | collective-permute-start | bytes 516104 | tf_op jit(solution)/shard_map/ppermute | solution.py:768
  385.7 14.6 %collective-permute-start.58 = (bf16[1,112,768]{2,1,0:T(8,128)(2,1)S(1)}, bf16[1,112,768]{2,1,0:T(8,128)(2,1)S(1)}, u32[]{:S(2)}, u32[]{:S(2)}) collective-permute-start(bf16[1,112,768]{2,1,0:T(8,128)(2,1)S(1)} %get-tuple-element.221), channel_id=1, source_target_pairs={{0,16},{4,20},{8,24},{12,28},{16,0},{20,4},{24,8},{28,12},{1,17},{... | collective-permute-start | bytes 516104 | tf_op jit(solution)/shard_map/ppermute | solution.py:768
  (42 other events, 701.8 us)
Sparse Core Ops, SparseCore 0:
  15.7 89.3 all-gather.2
